TPU v7x, 32 devices: a whole 2x2x4 slice. The times are simulated.
32 devices in a mesh: dp: 8 (over y, x, core), seq: 4 (over z).
Axes of the slice: x: 2, y: 2, z: 4, core: 2. Of those that a mesh axis runs over, the one named last changes fastest.
Arguments:
- inputs: bfloat16 [16384, 1024], P(('dp', 'seq')), may hold values from -6 to 6
- cotangent: bfloat16 [16384, 1024], P(('dp', 'seq')), may hold values from -6 to 6
- target_slot: int32 [16384], P(('dp', 'seq')), may hold values from 0 to 767, as said below
- anchor_slot: int32 [16384], P(('dp', 'seq')), may hold values from 0 to 767, as said below
- sequence_start: int32 [16384], P(('dp', 'seq')), may hold values from 0 to 2047, as said below
- attention_in: float32 [1024, 3072], P(('dp', 'seq')), may hold values from -0.09375 to 0.09375
- attention_out: float32 [1024, 1024], P(('dp', 'seq')), may hold values from -1.5 to 1.5
- gate_up: float32 [1024, 5632], P(('dp', 'seq')), may hold values from -0.09375 to 0.09375
- feed_down: float32 [2816, 1024], P(('dp', 'seq')), may hold values from -0.109375 to 0.109375
- norm_gains: float32 [2, 1024], P(None, ('dp', 'seq')), may hold values from 0.5 to 8
- first_in: float32 [1024, 3072], P(('dp', 'seq')), may hold values from -0.00048828125 to 0.00048828125
- first_out: float32 [1024, 1024], P(('dp', 'seq')), may hold values from -4.5776367e-05 to 4.5776367e-05
- first_gate: float32 [1024, 5632], P(('dp', 'seq')), may hold values from -0.00048828125 to 0.00048828125
- first_down: float32 [2816, 1024], P(('dp', 'seq')), may hold values from -0.00048828125 to 0.00048828125
- first_gains: float32 [2, 1024], P(None, ('dp', 'seq')), may hold values from -0.00048828125 to 0.00048828125
- second_in: float32 [1024, 3072], P(('dp', 'seq')), may hold values from 4.094308e-09 to 1.6346096e-08
- second_out: float32 [1024, 1024], P(('dp', 'seq')), may hold values from 4.094308e-11 to 1.6346097e-10
- second_gate: float32 [1024, 5632], P(('dp', 'seq')), may hold values from 4.094308e-09 to 1.6346096e-08
- second_down: float32 [2816, 1024], P(('dp', 'seq')), may hold values from 4.094308e-09 to 1.6346096e-08
- second_gains: float32 [2, 1024], P(None, ('dp', 'seq')), may hold values from 4.094308e-09 to 1.6346096e-08
Outputs:
- outputs: bfloat16 [16384, 1024], P(('dp', 'seq'))
- input_gradient: bfloat16 [16384, 1024], P(('dp', 'seq'))
- gradient_norm: float32 [], replicated
- updated_first_in: float32 [1024, 3072], P(('dp', 'seq'))
- updated_second_in: float32 [1024, 3072], P(('dp', 'seq'))
- updated_attention_in: float32 [1024, 3072], P(('dp', 'seq'))
- updated_first_out: float32 [1024, 1024], P(('dp', 'seq'))
- updated_second_out: float32 [1024, 1024], P(('dp', 'seq'))
- updated_attention_out: float32 [1024, 1024], P(('dp', 'seq'))
- updated_first_gate: float32 [1024, 5632], P(('dp', 'seq'))
- updated_second_gate: float32 [1024, 5632], P(('dp', 'seq'))
- updated_gate_up: float32 [1024, 5632], P(('dp', 'seq'))
- updated_first_down: float32 [2816, 1024], P(('dp', 'seq'))
- updated_second_down: float32 [2816, 1024], P(('dp', 'seq'))
- updated_feed_down: float32 [2816, 1024], P(('dp', 'seq'))
- updated_first_gains: float32 [2, 1024], P(None, ('dp', 'seq'))
- updated_second_gains: float32 [2, 1024], P(None, ('dp', 'seq'))
- updated_norm_gains: float32 [2, 1024], P(None, ('dp', 'seq'))
Inputs may be any that keep to these rules, and one draw needn't show every extreme that they name: `target_slot`: A device at seq index s sends its 512 rows to the owners of seq index s: value g * 96 + q is slot q of its block for dp index g. Values on one device are distinct and the used slots of a block are its first ones. Every owner receives 512 rows in all, and in every draw some device fills all 96 slots of some block. `anchor_slot`: value j * 96 + q: the row arrives from the device at dp index j of the same seq index, from slot q of its block for this owner; it matches target_slot, and each value stands once on a device. `sequence_start`: rows of one dp index form a group of 2048 rows in seq order; the value is the group position of the first row of the row's sequence, never above the row's own position and never falling within a group. A group holds three runs: a leading and a trailing one of 1 to 511 rows each (parts of sequences cut at the group's ends), and between them one whole sequence that begins on the first device of seq and ends on the last.
All inputs are finite; a program needn't handle non-finite values.
Results may differ from a plain program's by a relative error of at most 0.02.
Values may be sent and summed in bfloat16 or wider, within the bound.
No kernel may reach another device: no remote copies, remote signals or barrier semaphores. Data moves between devices by JAX's collectives and lax.ppermute only.
A program may use at most 256 MiB of HBM per device.

v0:
```python
import functools

import jax
import jax.numpy as jnp
from jax import lax
from jax.experimental import pallas as pl
from jax.experimental.pallas import tpu as pltpu
from jax.sharding import Mesh
from jax.sharding import PartitionSpec as P

D = 1024
HEAD = 64
FF = 2816
STEP = 10
LANES = 128

EPSILON = 1e-05
THETA = 500000.0
NEGATIVE = -1e30
BETA_FIRST = 0.9
BETA_SECOND = 0.95
ADAM_EPSILON = 1e-08
DECAY = 0.1
CLIP = 1.0
SCALE = 0.125
VMEM = 56 * 1024 * 1024
F32 = jnp.float32
BF16 = jnp.bfloat16
ROWS = ("chip", "core", "seq")


def norm_rows(values, gain_row):
    inverse = lax.rsqrt(jnp.mean(values * values, axis=1, keepdims=True) + EPSILON)
    normal = values * inverse
    return (normal * gain_row[None, :], normal, inverse)


def norm_back(upstream, normal, inverse, gain_row):
    gain_grad = jnp.sum(upstream * normal, axis=0)
    scaled = upstream * gain_row[None, :]
    return (
        inverse * (scaled - normal * jnp.mean(scaled * normal, axis=1, keepdims=True)),
        gain_grad,
    )


def rope_tables(positions):
    half_size = HEAD // 2
    frequency = jnp.power(THETA, -2.0 * jnp.arange(half_size, dtype=F32) / HEAD)
    angles = positions[:, None] * frequency[None, :]
    cosine = jnp.cos(angles)
    sine = jnp.sin(angles)
    return (
        jnp.concatenate([cosine] * 4, axis=1),
        jnp.concatenate([-sine, sine, -sine, sine], axis=1),
    )


def swap_halves(values):
    lane = lax.broadcasted_iota(jnp.int32, values.shape, 1)
    left = pltpu.roll(values, LANES - HEAD // 2, 1)
    right = pltpu.roll(values, HEAD // 2, 1)
    return jnp.where(lane % HEAD < HEAD // 2, left, right)


def contract_last(left, right):
    return lax.dot_general(left, right, (((1,), (1,)), ((), ())), preferred_element_type=F32)


def params():
    return pltpu.CompilerParams(vmem_limit_bytes=VMEM)


def turned(values):
    return values.astype(F32).T.astype(BF16)


def rows_at(index, count):
    return pl.ds(pl.multiple_of(index * count, count), count)


def project_kernel(spans, half, place_ref, x_ref, gain_ref, wa_ref, wb_ref, cos_ref, sin_ref, h_ref, *outs):
    step = pl.program_id(0)
    hw = wa_ref.shape[1]

    @pl.when(step == 0)
    def _():
        x = x_ref[...].astype(F32)
        inverse = lax.rsqrt(jnp.mean(x * x, axis=1, keepdims=True) + EPSILON)
        h_ref[...] = (x * inverse * gain_ref[...]).astype(BF16)

    def work(w_ref, rotated):
        acc = jnp.dot(h_ref[...], w_ref[...], preferred_element_type=F32)
        if rotated:
            pieces = []
            for c in range(hw // LANES):
                part = acc[:, c * LANES : (c + 1) * LANES]
                pieces.append(part * cos_ref[...] + swap_halves(part) * sin_ref[...])
            acc = jnp.concatenate(pieces, axis=1)
        low = acc.astype(BF16)
        for k in range(spans):

            @pl.when((step % spans) ^ place_ref[0] == k)
            def _(k=k):
                for pair in range(hw // LANES):
                    outs[pair * spans + k][...] = low[:, pair * LANES : (pair + 1) * LANES]

    turning = step < 2 * spans
    pl.when(step < half)(lambda: work(wa_ref, True))
    pl.when((step >= half) & turning)(lambda: work(wb_ref, True))
    pl.when(jnp.logical_not(turning))(lambda: work(wb_ref, False))


def project(spot, x, gain_row, weights, cosine, sine, spans):
    rows, width = x.shape
    hw = width // spans
    half = 3 * spans // 2
    fixed = lambda t, p: (0, 0)
    return pl.pallas_call(
        functools.partial(project_kernel, spans, half),
        grid_spec=pltpu.PrefetchScalarGridSpec(
            num_scalar_prefetch=1,
            grid=(3 * spans,),
            in_specs=[
                pl.BlockSpec((rows, width), fixed),
                pl.BlockSpec((1, width), fixed),
                pl.BlockSpec((width, hw), lambda t, p: (0, jnp.minimum(t, half - 1))),
                pl.BlockSpec((width, hw), lambda t, p: (0, jnp.maximum(t - half, 0))),
                pl.BlockSpec((rows, LANES), fixed),
                pl.BlockSpec((rows, LANES), fixed),
            ],
            out_specs=[pl.BlockSpec((rows, width), fixed)]
            + [pl.BlockSpec((rows, LANES), lambda t, p: (0, t // spans))] * (width // LANES),
        ),
        out_shape=[jax.ShapeDtypeStruct((rows, width), BF16)]
        + [jax.ShapeDtypeStruct((rows, 3 * LANES), BF16)] * (width // LANES),
        compiler_params=params(),
        cost_estimate=pl.CostEstimate(
            flops=17250000000, bytes_accessed=0, transcendentals=0
        ),
        name="project",
    )(spot, x, gain_row, *weights, cosine, sine)


def attend_kernel(spans, place_ref, start_ref, *refs):
    pieces, refs = refs[: 3 * spans], refs[3 * spans :]
    lows, (out_ref, log_ref, q_scr, k_scr, v_scr) = refs[:spans], refs[spans:]
    block = q_scr.shape[0] // spans
    here = place_ref[0]
    relative = pl.program_id(0)
    i = relative ^ here
    lane = lax.broadcasted_iota(jnp.int32, (block, LANES), 1)
    first = lane < HEAD

    @pl.when(relative == 0)
    def _():
        for k in range(spans):
            at = rows_at(here ^ k, block)
            q_scr[k * block : (k + 1) * block, :] = pieces[k][...]
            k_scr[at, :] = pieces[spans + k][...]
            v_scr[:, at] = turned(pieces[2 * spans + k][...])

    q_pair = q_scr[rows_at(relative, block), :] * SCALE
    key = lax.broadcasted_iota(jnp.int32, (block, block), 0)
    query = lax.broadcasted_iota(jnp.int32, (block, block), 1)
    starts = start_ref[:, rows_at(i, block)]
    heads = []
    for head in range(2):
        mine = first if head == 0 else jnp.logical_not(first)
        heads.append(jnp.where(mine, q_pair, jnp.zeros_like(q_pair)))

    def visit(j, carry, diagonal):
        at = rows_at(j, block)
        k = k_scr[at, :]
        seen = key + j * block >= starts
        if diagonal:
            seen = seen & (key <= query)
        result = []
        for head in range(2):
            s = jnp.where(seen, contract_last(k, heads[head]), NEGATIVE)
            lines = slice(head * HEAD, (head + 1) * HEAD)
            new = jnp.max(s, axis=0, keepdims=True)
            if not diagonal:
                top, total, acc = carry[head]
                new = jnp.maximum(top, new)
            p = jnp.exp(s - new)
            added = jnp.sum(p, axis=0, keepdims=True)
            weighed = jnp.dot(v_scr[lines, at], p.astype(BF16), preferred_element_type=F32)
            if not diagonal:
                factor = jnp.exp(top - new)
                added = added + total * factor
                weighed = weighed + acc * factor
            result.append((new, added, weighed))
        return tuple(result)

    carry = visit(i, None, True)
    carry = lax.fori_loop(0, i, lambda j, c: visit(j, c, False), carry)
    parts = []
    for head in range(2):
        top, total, acc = carry[head]
        parts.append(acc / total)
        log_ref[head : head + 1, :] = top + jnp.log(total)
    out = jnp.concatenate(parts, axis=0).T
    out_ref[0] = out
    low = out.astype(BF16)
    for k in range(spans):

        @pl.when(relative == k)
        def _(k=k):
            lows[k][...] = low


def piece_specs(rows, spans):
    return [
        pl.BlockSpec((rows, LANES), functools.partial(lambda part, i, s: (0, part), part))
        for part in range(3)
        for _ in range(spans)
    ]


def attend(spot, qkv, starts):
    spans = len(qkv)
    rows = qkv[0].shape[0]
    group = rows * spans
    return pl.pallas_call(
        functools.partial(attend_kernel, spans),
        grid_spec=pltpu.PrefetchScalarGridSpec(
            num_scalar_prefetch=1,
            grid=(spans,),
            in_specs=[pl.BlockSpec((1, group), lambda i, s: (0, 0))] + piece_specs(rows, spans),
            out_specs=[pl.BlockSpec((rows, LANES), lambda i, s: (0, 0))] * spans
            + [
                pl.BlockSpec((1, rows, LANES), lambda i, s: (i, 0, 0)),
                pl.BlockSpec((8, rows), lambda i, s: (0, i ^ s[0])),
            ],
            scratch_shapes=[
                pltpu.VMEM((group, LANES), BF16),
                pltpu.VMEM((group, LANES), BF16),
                pltpu.VMEM((LANES, group), BF16),
            ],
        ),
        out_shape=[jax.ShapeDtypeStruct((rows, LANES), BF16)] * spans
        + [
            jax.ShapeDtypeStruct((spans, rows, LANES), F32),
            jax.ShapeDtypeStruct((8, group), F32),
        ],
        compiler_params=params(),
        cost_estimate=pl.CostEstimate(
            flops=18400000000, bytes_accessed=0, transcendentals=0
        ),
        name="attend",
    )(spot, starts.reshape(1, group), *(list(qkv) * 3))


def attend_back_kernel(spans, place_ref, start_ref, *refs):
    pieces, refs = refs[: 3 * spans], refs[3 * spans :]
    grads, refs = refs[:spans], refs[spans:]
    (out_ref, log_ref, cos_ref, sin_ref), refs = refs[:4], refs[4:]
    outs, refs = refs[:spans], refs[spans:]
    q_scr, k_scr, v_scr, do_scr, dq_scr, dk_scr, dv_scr, delta_ref, turned_ref = refs
    block = q_scr.shape[0] // spans
    here = place_ref[0]
    j = pl.program_id(0)
    lane = lax.broadcasted_iota(jnp.int32, (block, LANES), 1)
    first = lane < HEAD

    @pl.when(j == 0)
    def _():
        for k in range(spans):
            at = rows_at(here ^ k, block)
            q_scr[at, :] = pieces[k][...]
            k_scr[at, :] = pieces[spans + k][...]
            v_scr[at, :] = pieces[2 * spans + k][...]
            do = grads[k][...]
            do_scr[at, :] = do
            product = (do.astype(F32) * out_ref[k]).T
            delta_ref[0:1, at] = jnp.sum(product[:HEAD], axis=0, keepdims=True)
            delta_ref[1:2, at] = jnp.sum(product[HEAD:], axis=0, keepdims=True)
        turned_ref[...] = jnp.zeros_like(turned_ref)

    now = rows_at(j, block)
    k_pair = k_scr[now, :]
    v_pair = v_scr[now, :]
    k_turned = turned(k_pair)
    key = j * block + lax.broadcasted_iota(jnp.int32, (block, block), 0)
    query = lax.broadcasted_iota(jnp.int32, (block, block), 1)

    def visit(i, carry, diagonal):
        dk, dv = carry
        at = rows_at(i, block)
        q_pair = q_scr[at, :] * SCALE
        do_pair = do_scr[at, :]
        seen = key >= start_ref[:, at]
        if diagonal:
            seen = seen & (key <= query + i * block)
        for head in range(2):
            mine = first if head == 0 else jnp.logical_not(first)
            q = jnp.where(mine, q_pair, jnp.zeros_like(q_pair))
            do = jnp.where(mine, do_pair, jnp.zeros_like(do_pair))
            s = jnp.where(seen, contract_last(k_pair, q), NEGATIVE)
            p = jnp.exp(s - log_ref[head : head + 1, at])
            dp = contract_last(v_pair, do)
            ds = (p * (dp - delta_ref[head : head + 1, at])).astype(BF16)
            dv = dv + jnp.dot(p.astype(BF16), do, preferred_element_type=F32)
            dk = dk + jnp.dot(ds, q, preferred_element_type=F32)
            lines = slice(head * HEAD, (head + 1) * HEAD)
            turned_ref[lines, at] += jnp.dot(k_turned[lines], ds, preferred_element_type=F32)
        return (dk, dv)

    zero = jnp.zeros((block, LANES), F32)
    carry = visit(j, (zero, zero), True)
    dk, dv = lax.fori_loop(j + 1, spans, lambda i, c: visit(i, c, False), carry)

    def turn_back(values, at):
        return values * cos_ref[at, :] + swap_halves(values * sin_ref[at, :])

    dk_scr[now, :] = turn_back(dk, now).astype(BF16)
    dv_scr[now, :] = dv.astype(BF16)

    @pl.when(j == spans - 1)
    def _():
        def finish(i, carry):
            at = rows_at(i, block)
            dq_scr[at, :] = turn_back(turned_ref[:, at].T * SCALE, at).astype(BF16)
            return carry

        lax.fori_loop(0, spans, finish, 0)
        for k in range(spans):
            at = rows_at(here ^ k, block)
            for part, scr in enumerate((dq_scr, dk_scr, dv_scr)):
                outs[k][:, part * LANES : (part + 1) * LANES] = scr[at, :]


def attend_back(spot, pair, qkv, starts, grads, out, logs, cosine, sine):
    spans = len(qkv)
    rows = qkv[0].shape[0]
    group = rows * spans
    whole = lambda j, s: (0, 0)
    low = pltpu.VMEM((group, LANES), BF16)
    return pl.pallas_call(
        functools.partial(attend_back_kernel, spans),
        grid_spec=pltpu.PrefetchScalarGridSpec(
            num_scalar_prefetch=1,
            grid=(spans,),
            in_specs=[pl.BlockSpec((1, group), whole)]
            + piece_specs(rows, spans)
            + [pl.BlockSpec((rows, LANES), lambda j, s: (0, pair))] * spans
            + [
                pl.BlockSpec((spans, rows, LANES), lambda j, s: (0, 0, 0)),
                pl.BlockSpec((8, group), whole),
                pl.BlockSpec((group, LANES), whole),
                pl.BlockSpec((group, LANES), whole),
            ],
            out_specs=[pl.BlockSpec((rows, 3 * LANES), whole)] * spans,
            scratch_shapes=[low] * 7 + [pltpu.VMEM((8, group), F32), pltpu.VMEM((LANES, group), F32)],
        ),
        out_shape=[jax.ShapeDtypeStruct((rows, 3 * LANES), BF16)] * spans,
        compiler_params=params(),
        cost_estimate=pl.CostEstimate(
            flops=27600000000, bytes_accessed=0, transcendentals=0
        ),
        name="attend_back",
    )(spot, starts.reshape(1, group), *(list(qkv) * 3), *grads, out, logs, cosine, sine)


def core_split(values, block, own):
    width = values.shape[1]
    sides = []
    for core in range(2):
        blocks = [values[:, b * block : (b + 1) * block] for b in range(core, width // block, 2)]
        sides.append(jnp.concatenate(blocks, axis=1))
    return (jnp.where(own == 0, sides[0], sides[1]), jnp.where(own == 0, sides[1], sides[0]))


def core_merge(mine, other, block, own):
    sides = (jnp.where(own == 0, mine, other), jnp.where(own == 0, other, mine))
    blocks = mine.shape[1] // block
    return jnp.concatenate(
        [side[:, b * block : (b + 1) * block] for b in range(blocks) for side in sides], axis=1
    )


def middle_kernel(spans, block, place_ref, x_ref, dy_ref, gain_ref, om_ref, oo_ref, *refs):
    heads = x_ref.shape[1] // LANES
    attended, refs = refs[:heads], refs[heads:]
    (gm_ref, um_ref, go_ref, uo_ref, da_ref, db_ref), refs = refs[:6], refs[6:]
    (y_ref, dx_ref, branch_ref, ow_ref, ox_ref, gain_grad_ref), refs = refs[:6], refs[6:]
    (gk_ref, uk_ref, gs_ref, us_ref, ga_ref, gb_ref), refs = refs[:6], refs[6:]
    grads, refs = refs[:spans], refs[spans:]
    hm_scr, ho_scr, kept_scr, sent_scr, x2_scr, y_scr, dm_scr, do_scr, wide_scr = refs
    step, steps = pl.program_id(0), pl.num_programs(0)
    half = x_ref.shape[1] // 2
    here, core = place_ref[0], place_ref[1]

    def pieces_at(pieces):
        for index, piece in enumerate(pieces):
            pair, k = index // spans, index % spans
            yield rows_at((here ^ k) * (heads // spans) + pair, LANES), piece

    hw = x_ref.shape[1] // spans

    def normal():
        x2 = x2_scr[...]
        inverse = lax.rsqrt(jnp.mean(x2 * x2, axis=1, keepdims=True) + EPSILON)
        return (x2 * inverse, inverse)

    @pl.when(step == 0)
    def _():
        for at, piece in pieces_at(attended):
            wide_scr[:, at] = piece[...]
        mine, other = core_split(wide_scr[...], block, core)
        ow_ref[...] = mine
        ox_ref[...] = other
        x2_scr[...] = (
            x_ref[...].astype(F32)
            + jnp.dot(mine, om_ref[...], preferred_element_type=F32)
            + jnp.dot(other, oo_ref[...], preferred_element_type=F32)
        )
        h = (normal()[0] * gain_ref[...]).astype(BF16).astype(F32)
        mine, other = core_split(h, block, core)
        hm_scr[...] = mine.astype(BF16)
        ho_scr[...] = other.astype(BF16)
        kept_scr[...] = mine.T.astype(BF16)
        sent_scr[...] = other.T.astype(BF16)
        y_scr[...] = jnp.zeros_like(y_scr)
        dm_scr[...] = jnp.zeros_like(dm_scr)
        do_scr[...] = jnp.zeros_like(do_scr)

    hm, ho, dy = hm_scr[...], ho_scr[...], dy_ref[...]
    gm, um, go, uo = gm_ref[...], um_ref[...], go_ref[...], uo_ref[...]
    gate = jnp.dot(hm, gm, preferred_element_type=F32) + jnp.dot(ho, go, preferred_element_type=F32)
    up = jnp.dot(hm, um, preferred_element_type=F32) + jnp.dot(ho, uo, preferred_element_type=F32)
    share = jax.nn.sigmoid(gate)
    active = gate * share
    hidden_full = active * up
    hidden = hidden_full.astype(BF16)
    down = jnp.concatenate([da_ref[...], db_ref[...]], axis=1)
    y_scr[...] += jnp.dot(hidden, down, preferred_element_type=F32)
    dhid = contract_last(dy, down)
    dgate = (dhid * up * share * (1.0 + gate * (1.0 - share))).astype(BF16)
    dup = (dhid * active).astype(BF16)
    dm_scr[...] += contract_last(dgate, gm) + contract_last(dup, um)
    do_scr[...] += contract_last(dgate, go) + contract_last(dup, uo)
    kept, sent = kept_scr[...], sent_scr[...]
    gs_ref[...] = jnp.dot(sent, dgate, preferred_element_type=F32).astype(BF16)
    us_ref[...] = jnp.dot(sent, dup, preferred_element_type=F32).astype(BF16)
    gk_ref[...] = jnp.dot(kept, dgate, preferred_element_type=F32).astype(BF16)
    uk_ref[...] = jnp.dot(kept, dup, preferred_element_type=F32).astype(BF16)
    hidden_turned = hidden_full.T.astype(BF16)
    ga_ref[...] = jnp.dot(hidden_turned, dy[:, :half], preferred_element_type=F32).astype(BF16)
    gb_ref[...] = jnp.dot(hidden_turned, dy[:, half:], preferred_element_type=F32).astype(BF16)

    @pl.when(step == steps - 1)
    def _():
        y_ref[...] = (x2_scr[...] + y_scr[...]).astype(BF16)
        norm, inverse = normal()
        dh = core_merge(dm_scr[...], do_scr[...], block, core)
        gain_grad_ref[...] = jnp.sum(dh * norm, axis=0, keepdims=True)
        scaled = dh * gain_ref[...]
        inner = jnp.mean(scaled * norm, axis=1, keepdims=True)
        dx = dy_ref[...].astype(F32) + inverse * (scaled - norm * inner)
        dx_ref[...] = dx
        branch = dx.astype(BF16)
        branch_ref[...] = branch
        mine = contract_last(branch, om_ref[...]).astype(BF16)
        other = contract_last(branch, oo_ref[...]).astype(BF16)
        wide_scr[...] = core_merge(mine, other, block, core)
        for k in range(spans):
            grads[k][...] = wide_scr[:, rows_at(here ^ k, hw)]


def middle(spot, owners, spans, x, dy, gain_row, weight_out, attended, weight_gate, weight_down):
    rows, width = x.shape
    hidden = weight_gate[0].shape[1]
    heads, half, tile = width // LANES, width // 2, 2 * LANES
    tiles = hidden // tile
    fixed = lambda t, s: (0, 0)
    full = pl.BlockSpec((rows, width), fixed)
    side = pl.BlockSpec((rows, half), fixed)
    across = lambda t, s: (0, t)
    along = lambda t, s: (t, 0)
    shape = jax.ShapeDtypeStruct
    return pl.pallas_call(
        functools.partial(middle_kernel, spans, width // owners),
        grid_spec=pltpu.PrefetchScalarGridSpec(
            num_scalar_prefetch=1,
            grid=(tiles,),
            in_specs=[full, full, pl.BlockSpec((1, width), fixed)]
            + [pl.BlockSpec((half, width), fixed)] * 2
            + [pl.BlockSpec((rows, LANES), fixed)] * heads
            + [pl.BlockSpec((half, tile), across)] * 4
            + [pl.BlockSpec((tile, half), along)] * 2,
            out_specs=[full] * 3
            + [side] * 2
            + [pl.BlockSpec((1, width), fixed)]
            + [pl.BlockSpec((half, tile), across)] * 4
            + [pl.BlockSpec((tile, half), along)] * 2
            + [pl.BlockSpec((rows, width // spans), fixed)] * spans,
            scratch_shapes=[
                pltpu.VMEM((rows, half), BF16),
                pltpu.VMEM((rows, half), BF16),
                pltpu.VMEM((half, rows), BF16),
                pltpu.VMEM((half, rows), BF16),
                pltpu.VMEM((rows, width), F32),
                pltpu.VMEM((rows, width), F32),
                pltpu.VMEM((rows, half), F32),
                pltpu.VMEM((rows, half), F32),
                pltpu.VMEM((rows, width), BF16),
            ],
        ),
        out_shape=[
            shape((rows, width), BF16),
            shape((rows, width), F32),
            shape((rows, width), BF16),
            shape((rows, half), BF16),
            shape((rows, half), BF16),
            shape((1, width), F32),
        ]
        + [shape((half, hidden), BF16)] * 4
        + [shape((hidden, half), BF16)] * 2
        + [shape((rows, width // spans), BF16)] * spans,
        compiler_params=params(),
        cost_estimate=pl.CostEstimate(
            flops=55200000000, bytes_accessed=0, transcendentals=0
        ),
        name="middle",
    )(
        spot,
        x,
        dy,
        gain_row,
        *weight_out,
        *attended,
        *weight_gate,
        *weight_down,
    )


def last_kernel(spans, half, block, place_ref, x_ref, dx2_ref, gain_ref, second_ref, h_ref, wa_ref, wb_ref, *refs):
    heads = x_ref.shape[1] // LANES
    pieces, refs = refs[:heads], refs[heads:]
    sa_ref, sb_ref, ka_ref, kb_ref, dx_ref, gk_ref, gs_ref, d_scr, kept_scr, sent_scr, dh_scr = refs
    step = pl.program_id(0)

    @pl.when(step == 0)
    def _():
        kept, sent = core_split(h_ref[...].astype(F32), block, place_ref[1])
        kept_scr[...] = kept.T.astype(BF16)
        sent_scr[...] = sent.T.astype(BF16)
        dh_scr[...] = jnp.zeros_like(dh_scr)

    for k in range(spans):

        @pl.when((step % spans) ^ place_ref[0] == k)
        def _(k=k):
            for pair in range(heads // spans):
                d_scr[:, pair * LANES : (pair + 1) * LANES] = pieces[pair * spans + k][...]

    def work(w_ref, s_ref, k_ref):
        d = d_scr[...]
        s_ref[...] = jnp.dot(sent_scr[...], d, preferred_element_type=F32).astype(BF16)
        k_ref[...] = jnp.dot(kept_scr[...], d, preferred_element_type=F32).astype(BF16)
        dh_scr[...] += contract_last(d, w_ref[...])

    pl.when(step < half)(lambda: work(wa_ref, sa_ref, ka_ref))
    pl.when(step >= half)(lambda: work(wb_ref, sb_ref, kb_ref))

    @pl.when(step == pl.num_programs(0) - 1)
    def _():
        x = x_ref[...].astype(F32)
        inverse = lax.rsqrt(jnp.mean(x * x, axis=1, keepdims=True) + EPSILON)
        norm = x * inverse
        dh = dh_scr[...]
        row = lax.broadcasted_iota(jnp.int32, (LANES, x.shape[1]), 0)
        gains = jnp.where(row == 0, jnp.sum(dh * norm, axis=0, keepdims=True), 0.0)
        gains = jnp.where(row == 1, second_ref[...], gains)
        kept, sent = core_split(gains, block, place_ref[1])
        gk_ref[...] = kept.T.astype(BF16)
        gs_ref[...] = sent.T.astype(BF16)
        scaled = dh * gain_ref[...]
        inner = jnp.mean(scaled * norm, axis=1, keepdims=True)
        dx_ref[...] = (dx2_ref[...] + inverse * (scaled - norm * inner)).astype(BF16)


def last(spot, owners, spans, x, dx2, gain_row, gain_two_grad, normed, weights, pieces):
    rows, width = x.shape
    hw = width // spans
    half = 3 * spans // 2
    low = lambda t, s: (0, jnp.minimum(t, half - 1))
    high = lambda t, s: (0, jnp.maximum(t - half, 0))
    fixed = lambda t, s: (0, 0)
    full = pl.BlockSpec((rows, width), fixed)
    row = pl.BlockSpec((1, width), fixed)
    shape = jax.ShapeDtypeStruct
    return pl.pallas_call(
        functools.partial(last_kernel, spans, half, width // owners),
        grid_spec=pltpu.PrefetchScalarGridSpec(
            num_scalar_prefetch=1,
            grid=(3 * spans,),
            in_specs=[full, full, row, row, full]
            + [pl.BlockSpec((width, hw), low), pl.BlockSpec((width, hw), high)]
            + [pl.BlockSpec((rows, LANES), lambda t, s: (0, t // spans))] * len(pieces),
            out_specs=[
                pl.BlockSpec((width // 2, hw), low),
                pl.BlockSpec((width // 2, hw), high),
                pl.BlockSpec((width // 2, hw), low),
                pl.BlockSpec((width // 2, hw), high),
                full,
                pl.BlockSpec((width // 2, LANES), fixed),
                pl.BlockSpec((width // 2, LANES), fixed),
            ],
            scratch_shapes=[
                pltpu.VMEM((rows, hw), BF16),
                pltpu.VMEM((width // 2, rows), BF16),
                pltpu.VMEM((width // 2, rows), BF16),
                pltpu.VMEM((rows, width), F32),
            ],
        ),
        out_shape=[shape((width // 2, 3 * width // 2), BF16)] * 4
        + [shape((rows, width), BF16)]
        + [shape((width // 2, LANES), BF16)] * 2,
        compiler_params=params(),
        cost_estimate=pl.CostEstimate(
            flops=21850000000, bytes_accessed=0, transcendentals=0
        ),
        name="last",
    )(spot, x, dx2, gain_row, gain_two_grad, normed, *weights, *pieces)


def adamw(weight, gradient, first, second, rate, factor):
    clipped = gradient * factor
    first_new = BETA_FIRST * first + (1.0 - BETA_FIRST) * clipped
    second_new = BETA_SECOND * second + (1.0 - BETA_SECOND) * clipped * clipped
    corrected_first = first_new / (1.0 - BETA_FIRST**STEP)
    corrected_second = second_new / (1.0 - BETA_SECOND**STEP)
    weight_new = weight - rate * (
        corrected_first / (jnp.sqrt(corrected_second) + ADAM_EPSILON) + DECAY * weight
    )
    return (first_new, second_new, weight_new)


def swap(values, axis, step):
    count = lax.axis_size(axis)
    return lax.ppermute(values, axis, [(i, i ^ step) for i in range(count)])


def paired():
    return lax.axis_size("seq") == 4


def group_place():
    if paired():
        return 2 * lax.axis_index("core") + lax.axis_index("seq") % 2
    return lax.axis_index("seq")


def group_swap(values, step):
    if not paired():
        return swap(values, "seq", step)
    spans = lax.axis_size("seq")
    pairs = [
        (c * spans + z, (c ^ (step >> 1)) * spans + (z ^ (step & 1)))
        for c in range(2)
        for z in range(spans)
    ]
    return lax.ppermute(values, ("core", "seq"), pairs)


def regroup(values, *gates):
    if not paired():
        return values
    spans = lax.axis_size("seq")
    pairs = [
        (c * spans + z, (z // 2) * spans + 2 * c + z % 2)
        for c in range(2)
        for z in range(spans)
        if c != z // 2
    ]
    stays = lax.axis_index("core") == lax.axis_index("seq") // 2
    came = after(lax.ppermute(values, ("core", "seq"), pairs), gates)
    return jnp.where(stays, values, came)


def trade(pieces, *gates):
    return [pieces[0], *after([group_swap(pieces[k], k) for k in range(1, len(pieces))], gates)]


def bit_of(axis, step):
    return lax.axis_index(axis) & step


def ordered(own_bit, mine, other, at):
    return jnp.where(own_bit == 0, jnp.stack([mine, other], at), jnp.stack([other, mine], at))


def in_order(pieces, here):
    count = len(pieces)
    bits = count.bit_length() - 1
    stack = jnp.stack(pieces).reshape((2,) * bits + pieces[0].shape)
    for at in range(bits):
        flipped = jnp.flip(stack, axis=at)
        stack = jnp.where((here >> (bits - 1 - at)) & 1 == 1, flipped, stack)
    return stack.reshape((count,) + pieces[0].shape)


def chip_bits():
    count = lax.axis_size("chip")
    bits = [b for b in range(count.bit_length() - 1)]
    return bits, bits[::-1]


def halves_of(values):
    middle = values.shape[-1] // 2
    return (values[..., :middle], values[..., middle:])


def spread(values, axes):
    count = 1
    for axis in axes:
        count *= lax.axis_size(axis)
    copies = jnp.broadcast_to(values[None], (count,) + values.shape)
    return lax.all_to_all(copies, axes, split_axis=0, concat_axis=0, tiled=True)


def gather_line(shard, *gates):
    spans = lax.axis_size("seq")
    pieces = [shard] + [swap(shard, "seq", k) for k in range(1, spans)]
    pieces = after(pieces, gates)
    return in_order(pieces, lax.axis_index("seq")).reshape(-1, shard.shape[1])


def after(values, *tokens):
    return lax.optimization_barrier((values, tokens))[0]


def gather_chips(block, gate=None, came=()):
    parts, orders = halves_of(block), chip_bits()
    for at_step in range(len(orders[0])):
        if gate is not None and at_step == len(orders[0]) - 1:
            parts = after(parts, gate)
        others = [swap(half, "chip", 1 << order[at_step]) for half, order in zip(parts, orders)]
        if at_step < len(came):
            others = after(others, came[at_step])
        parts = [
            ordered(
                bit_of("chip", 1 << order[at_step]),
                half,
                other,
                sum(1 for d in order[:at_step] if d > order[at_step]),
            )
            for half, other, order in zip(parts, others, orders)
        ]
    return [half.reshape(-1, half.shape[-1]) for half in parts]


def core_order(mine, other):
    chips, width = lax.axis_size("chip"), mine.shape[1]
    mine, other = mine.reshape(chips, -1, width), other.reshape(chips, -1, width)
    return ordered(lax.axis_index("core"), mine, other, 1).reshape(-1, width)


def core_sum(kept, sent, *gates):
    came = after([swap(other, "core", 1) for other in sent], gates)
    parts = [
        (mine.astype(F32) + other.astype(F32)).astype(BF16) for mine, other in zip(kept, came)
    ]
    return jnp.concatenate(parts, axis=-1)


def chips_scatter(values):
    return lax.psum_scatter(values, "chip", scatter_dimension=0, tiled=True)


def line_scatter(values):
    return lax.psum_scatter(values, "seq", scatter_dimension=0, tiled=True).astype(F32)


def direct_sum(values, axis, *gates):
    count, here = lax.axis_size(axis), lax.axis_index(axis)
    total = lax.dynamic_index_in_dim(values, here, 0, keepdims=False).astype(F32)
    pieces = [
        swap(lax.dynamic_index_in_dim(values, here ^ k, 0, keepdims=False), axis, k)
        for k in range(1, count)
    ]
    for piece in after(pieces, gates):
        total = total + piece.astype(F32)
    return total


def line_sum(values):
    spans = lax.axis_size("seq")
    return direct_sum(values.reshape(spans, -1, values.shape[-1]), "seq")


def chips_sum(values, *gates):
    chips = lax.axis_size("chip")
    return direct_sum(values.reshape(chips, -1, values.shape[-1]), "chip", *gates).astype(BF16)


def outer(left, right):
    return lax.dot_general(left, right, (((0,), (0,)), ((), ())), preferred_element_type=F32)


def row_parts(gradient):
    width = gradient.shape[1]
    chips = lax.axis_size("chip")
    parts = gradient.reshape(chips, 2, -1, width)
    own = lax.axis_index("core") == 0
    kept = jnp.where(own, parts[:, 0], parts[:, 1]).reshape(-1, width)
    sent = jnp.where(own, parts[:, 1], parts[:, 0]).reshape(-1, width)
    return (kept, sent)


def place(index, values, slots):
    chosen = lax.broadcasted_iota(jnp.int32, (slots, index.shape[0]), 0) == index[None, :]
    return jnp.dot(chosen.astype(BF16), values, preferred_element_type=F32).astype(BF16)


def pick(index, values):
    slots = values.shape[0]
    chosen = lax.broadcasted_iota(jnp.int32, (index.shape[0], slots), 1) == index[:, None]
    return jnp.dot(chosen.astype(BF16), values, preferred_element_type=F32).astype(BF16)


def per_device(
    inputs,
    cotangent,
    target_slot,
    anchor_slot,
    sequence_start,
    attention_in,
    attention_out,
    gate_up,
    feed_down,
    norm_gains,
    first_in,
    first_out,
    first_gate,
    first_down,
    first_gains,
    second_in,
    second_out,
    second_gate,
    second_down,
    second_gains,
):
    owners = lax.axis_size("chip") * lax.axis_size("core")
    spans = lax.axis_size("seq")
    rows, width = inputs.shape
    per_owner = rows // owners
    capacity = per_owner + per_owner // 2
    slots = owners * capacity
    group = rows * spans
    here = group_place()
    device = (lax.axis_index("chip") * 2 + lax.axis_index("core")) * spans + lax.axis_index("seq")
    spot = jnp.stack([here, lax.axis_index("core")]).astype(jnp.int32)

    def exchange(values):
        return lax.all_to_all(values, ("chip", "core"), split_axis=0, concat_axis=0, tiled=True)

    pairs = width // spans // LANES

    def by_pair(pieces):
        return [pieces[p * spans : (p + 1) * spans] for p in range(pairs)]

    def joined(lists):
        return [piece for pieces in lists for piece in pieces]

    columns = norm_gains.shape[1]
    own_gains = jnp.pad(norm_gains.astype(BF16).reshape(1, -1), ((0, 7), (0, width - 2 * columns)))
    placed = jnp.concatenate(
        [
            place(target_slot, inputs, slots).reshape(owners, capacity, width),
            jnp.broadcast_to(own_gains[None], (owners, 8, width)),
        ],
        axis=1,
    )
    arrived = exchange(placed)
    gains_line = arrived[:, capacity, : 2 * columns]
    arrived = arrived[:, :capacity].reshape(slots, width)
    line_in = gather_line(attention_in.astype(BF16), placed)
    picked = pick(anchor_slot, arrived)
    balanced_in = regroup(picked)
    line_gate = gather_line(gate_up.astype(BF16), picked)
    side_in = gather_chips(line_in, gate=picked)
    line_gate_late = after(line_gate, side_in, balanced_in)
    core_in = after(side_in, line_gate)
    own_starts = regroup(sequence_start.reshape(1, rows), side_in)
    straight = jnp.concatenate([attention_out.astype(BF16), feed_down.astype(BF16)], axis=0)
    side_rest = lax.all_gather(after(straight, side_in), ("chip", "seq"), axis=0, tiled=True)
    weight_in = [core_order(half, swap(half, "core", 1)) for half in core_in]
    gains_line = after(gains_line.astype(F32), side_in)
    gain_pieces = [gains_line] + [swap(gains_line, "seq", k) for k in range(1, spans)]
    gain_rows = in_order(gain_pieces, lax.axis_index("seq")).reshape(spans, owners, 2, columns)
    gain_rows = jnp.transpose(gain_rows, (2, 1, 0, 3)).reshape(2, width)

    own_starts = after(own_starts, balanced_in).reshape(rows)
    local = here * rows + jnp.arange(rows, dtype=jnp.int32) - own_starts
    cosine, sine = rope_tables(local.astype(F32))

    normed_one, *cut = project(spot, balanced_in, gain_rows[0:1], weight_in, cosine, sine, spans)
    cuts = by_pair(cut)
    qkv = [trade(cuts[0])]
    pieces = trade([own_starts.reshape(1, rows)] * spans, normed_one)
    starts = in_order(pieces, here).reshape(group)
    late = after(cotangent, normed_one)
    arrived_late = exchange(place(target_slot, late, slots))
    upstream = pick(anchor_slot, arrived_late)
    own_rows = attention_out.shape[0]

    def cut_rest(rest):
        rest = rest.reshape(-1, straight.shape[0], width)
        return [rest[:, :own_rows].reshape(-1, width), rest[:, own_rows:].reshape(-1, width)]

    forward = [attend(spot, after(qkv[0], upstream), starts)]
    upstream = regroup(upstream)
    positions = jnp.arange(group, dtype=jnp.int32) - after(starts, forward[0])
    cosine_all, sine_all = rope_tables(positions.astype(F32))
    side_rest = after(side_rest, forward[0])
    other_rest = swap(side_rest, "core", 1)
    side_rest = cut_rest(side_rest)
    for pieces in cuts[1:]:
        qkv.append(trade(pieces, forward[0]))
        forward.append(attend(spot, after(qkv[-1], upstream, side_rest), starts))
    side_gate = gather_chips(line_gate_late, came=(normed_one, forward[-1]))
    other_rest = cut_rest(after(other_rest, forward[-1]))
    weight_out = (side_rest[0], other_rest[0])
    weight_down = halves_of(core_order(side_rest[1], other_rest[1]))
    traded = [trade(out[:spans]) for out in forward]
    side_gate = after(side_gate, traded)
    weight_gate = side_gate + [swap(half, "core", 1) for half in side_gate]
    (
        result_low,
        middle_grad,
        branch_grad,
        attended_mine,
        attended_other,
        gain_two_grad,
        *rest,
    ) = middle(
        spot,
        owners,
        spans,
        balanced_in,
        upstream,
        gain_rows[1:2],
        weight_out,
        joined(traded),
        weight_gate,
        weight_down,
    )
    gate_kept, gate_sent, down_grad, grad_cut = rest[:2], rest[2:4], rest[4:6], rest[6:]
    grad_heads = trade(grad_cut)
    gate_both = core_sum(gate_kept, gate_sent, grad_heads)
    down_both = core_sum(*zip(*(row_parts(half) for half in down_grad)), grad_heads)
    grad_heads = after(grad_heads, gate_both, down_both)
    down_line = chips_scatter(down_both)
    gate_line = chips_scatter(gate_both)
    grads = [
        attend_back(spot, p, qkv[p], starts, grad_heads, *forward[p][spans:], cosine_all, sine_all)
        for p in range(pairs)
    ]
    result_slots = place(anchor_slot, after(regroup(result_low, grads[0]), grads[-1]), slots)
    outputs = exchange(result_slots)
    attended_mine, attended_other, branch_grad = after(
        (attended_mine, attended_other, branch_grad), grads[-1]
    )
    out_kept = outer(attended_mine, branch_grad).astype(BF16)
    out_sent = outer(attended_other, branch_grad).astype(BF16)
    middle_grad = after(middle_grad, result_slots, out_kept, out_sent, down_line)
    sent_a, sent_b, kept_a, kept_b, input_low, gains_kept, gains_sent = last(
        spot,
        owners,
        spans,
        balanced_in,
        middle_grad,
        gain_rows[0:1],
        gain_two_grad,
        normed_one,
        weight_in,
        joined(trade(pieces) for pieces in grads),
    )
    gate_shard = line_scatter(gate_line)
    down_shard = line_scatter(after(down_line, gate_shard))
    in_both = core_sum(
        [kept_a, kept_b, out_kept, gains_kept], [sent_a, sent_b, out_sent, gains_sent]
    )
    in_both = after(in_both, gate_line)
    in_line = chips_sum(in_both)
    outputs = pick(target_slot, after(outputs, in_both))
    shards = line_sum(in_line)
    in_shard, out_shard = shards[:, : 3 * width], shards[:, 3 * width : 4 * width]
    chosen = jnp.eye(2, LANES, dtype=F32)
    gain_shard = lax.dot_general(
        chosen,
        shards[:, 4 * width :],
        (((1,), (1,)), ((), ())),
        precision=lax.Precision.HIGHEST,
        preferred_element_type=F32,
    )
    returned = exchange(place(anchor_slot, regroup(input_low, in_both), slots))
    input_gradient = pick(target_slot, returned)
    local_total = (
        jnp.sum(in_shard * in_shard)
        + jnp.sum(out_shard * out_shard)
        + jnp.sum(gate_shard * gate_shard)
        + jnp.sum(down_shard * down_shard)
        + jnp.sum(gain_shard * gain_shard)
    )
    total = jnp.sum(spread(jnp.broadcast_to(local_total, (8, LANES)), ROWS).reshape(-1, 8, LANES)[:, 0, 0])
    gradient_norm = jnp.sqrt(total)
    factor = CLIP / jnp.maximum(gradient_norm, CLIP)
    updates = []
    for weight, gradient, first, second, rate in (
        (attention_in, in_shard, first_in, second_in, D ** (-0.5)),
        (attention_out, out_shard, first_out, second_out, 0.5),
        (gate_up, gate_shard, first_gate, second_gate, D ** (-0.5)),
        (feed_down, down_shard, first_down, second_down, 2.0 * FF ** (-0.5)),
        (norm_gains, gain_shard, first_gains, second_gains, 1.5),
    ):
        updates.extend(adamw(weight, gradient, first, second, rate, factor))
    return (outputs, input_gradient, gradient_norm, *updates)


def solution(mesh):
    owners, spans = mesh.shape["dp"], mesh.shape["seq"]
    parts = Mesh(mesh.devices.reshape(owners // 2, 2, spans), ROWS)
    rows = P(ROWS, None)
    columns = P(None, ROWS)
    line = P(ROWS)
    in_specs = (rows, rows, line, line, line) + ((rows,) * 4 + (columns,)) * 3
    out_specs = (rows, rows, P()) + (rows,) * 12 + (columns,) * 3
    return jax.shard_map(
        per_device, mesh=parts, in_specs=in_specs, out_specs=out_specs, check_vma=False
    )
```

profile of v0, /device:TPU:0, one launch (start us, length us, event | category | flops | bytes accessed | tf_op | source)
XLA Modules:
  0.0 605.7 jit_solution(15138250280758096838)
XLA Ops:
  21.2 7.4 %collective-permute-done.2 = bf16[32,3072]{1,0:T(8,128)(2,1)S(1)} collective-permute-done((bf16[32,3072]{1,0:T(8,128)(2,1)S(1)}, bf16[32,3072]{1,0:T(8,128)(2,1)S(1)}, u32[]{:S(2)}, u32[]{:S(2)}) %collective-permute-start.2) | collective-permute-done | bytes 196640 | tf_op jit(solution)/shard_map/ppermute | solution.py:644
  41.1 10.1 %collective-permute-done.4 = bf16[128,1536]{1,0:T(8,128)(2,1)} collective-permute-done((bf16[128,1536]{1,0:T(8,128)(2,1)}, bf16[128,1536]{1,0:T(8,128)(2,1)}, u32[]{:S(2)}, u32[]{:S(2)}) %collective-permute-start.4) | collective-permute-done | bytes 393248 | tf_op jit(solution)/shard_map/ppermute | solution.py:644
  67.4 9.3 %collective-permute-done.6 = bf16[2,128,1536]{2,1,0:T(8,128)(2,1)S(1)} collective-permute-done((bf16[2,128,1536]{2,1,0:T(8,128)(2,1)S(1)}, bf16[2,128,1536]{2,1,0:T(8,128)(2,1)S(1)}, u32[]{:S(2)}, u32[]{:S(2)}) %collective-permute-start.6) | collective-permute-done | bytes 786464 | tf_op jit(solution)/shard_map/ppermute | solution.py:644
  113.3 15.1 %project.1 = (bf16[512,1024]{1,0:T(8,128)(2,1)}, bf16[512,384]{1,0:T(8,128)(2,1)}, bf16[512,384]{1,0:T(8,128)(2,1)}, bf16[512,384]{1,0:T(8,128)(2,1)}, bf16[512,...) custom-call(s32[2]{0:T(128)} %pad_add_fusion.1.place_ref, ...), custom_call_target="tpu_custom_call" | custom-call | flops 17250000896 | tf_op jit(solution)/shard_map/project/pallas_call | solution.py:119
  145.8 12.4 %collective-permute-done.21.refs_1_.refs_5_.refs_9_ = bf16[512,384]{1,0:T(8,128)(2,1)} collective-permute-done((bf16[512,384]{1,0:T(8,128)(2,1)}, bf16[512,384]{1,0:T(8,128)(2,1)}, u32[]{:S(2)}, u32[]{:S(2)}) %collective-permute-start.21) | collective-permute-done | bytes 393248 | tf_op jit(solution)/shard_map/ppermute | solution.py:666
  158.2 10.9 %collective-permute-done.23.refs_3_.refs_7_.refs_11_ = bf16[512,384]{1,0:T(8,128)(2,1)} collective-permute-done((bf16[512,384]{1,0:T(8,128)(2,1)}, bf16[512,384]{1,0:T(8,128)(2,1)}, u32[]{:S(2)}, u32[]{:S(2)}) %collective-permute-start.23) | collective-permute-done | bytes 393248 | tf_op jit(solution)/shard_map/ppermute | solution.py:666
  173.5 15.6 %attend.2 = (bf16[512,128]{1,0:T(8,128)(2,1)}, bf16[512,128]{1,0:T(8,128)(2,1)}, bf16[512,128]{1,0:T(8,128)(2,1)}, bf16[512,128]{1,0:T(8,128)(2,1)}, f32[4,512,128]{2,1,0:T(8,128)}, /*index=5*/f32[8,2048]{1,0:T(8,128)}) custom-call(s32[2]{0:T(128)} %pad_add_fusion.1.place_ref, s32[1,2048]{1,0:T(1,128)} %reshape_reshape_reshape.2.start_ref, ...), custom_call_target="tpu_custom_call" | custom-call | flops 18400000000 | tf_op jit(solution)/shard_map/attend/pallas_call | solution.py:225
  190.6 6.2 %collective-permute-done.25.refs_1_.refs_5_.refs_9_ = bf16[512,384]{1,0:T(8,128)(2,1)} collective-permute-done((bf16[512,384]{1,0:T(8,128)(2,1)}, bf16[512,384]{1,0:T(8,128)(2,1)}, u32[]{:S(2)}, u32[]{:S(2)}) %collective-permute-start.25) | collective-permute-done | bytes 393248 | tf_op jit(solution)/shard_map/ppermute | solution.py:666
  198.2 5.9 collective-permute-done.27.refs_3_.refs_7_.refs_11_
  213.9 15.6 %attend.3 = (bf16[512,128]{1,0:T(8,128)(2,1)}, bf16[512,128]{1,0:T(8,128)(2,1)}, bf16[512,128]{1,0:T(8,128)(2,1)}, bf16[512,128]{1,0:T(8,128)(2,1)}, f32[4,512,128]{2,1,0:T(8,128)}, /*index=5*/f32[8,2048]{1,0:T(8,128)}) custom-call(s32[2]{0:T(128)} %pad_add_fusion.1.place_ref, s32[1,2048]{1,0:T(1,128)} %reshape_reshape_reshape.2.start_ref, ...), custom_call_target="tpu_custom_call" | custom-call | flops 18400000000 | tf_op jit(solution)/shard_map/attend/pallas_call | solution.py:225
  231.0 7.6 %collective-permute-done.36 = bf16[2,128,2816]{2,1,0:T(8,128)(2,1)} collective-permute-done((bf16[2,128,2816]{2,1,0:T(8,128)(2,1)}, bf16[2,128,2816]{2,1,0:T(8,128)(2,1)}, u32[]{:S(2)}, u32[]{:S(2)}) %collective-permute-start.36) | collective-permute-done | bytes 1441824 | tf_op jit(solution)/shard_map/ppermute | solution.py:644
  260.8 48.9 %middle.1 = (bf16[512,1024]{1,0:T(8,128)(2,1)}, f32[512,1024]{1,0:T(8,128)}, bf16[512,1024]{1,0:T(8,128)(2,1)}, bf16[512,512]{1,0:T(8,128)(2,1)}, bf16[512,512]{...) custom-call(s32[2]{0:T(128)} %pad_add_fusion.1.place_ref, ...), custom_call_target="tpu_custom_call" | custom-call | flops 55199997952 | tf_op jit(solution)/shard_map/middle/pallas_call | solution.py:483
  315.5 7.0 %collective-permute-done.41.refs_13_ = bf16[512,256]{1,0:T(8,128)(2,1)S(1)} collective-permute-done((bf16[512,256]{1,0:T(8,128)(2,1)S(1)}, bf16[512,256]{1,0:T(8,128)(2,1)S(1)}, u32[]{:S(2)}, u32[]{:S(2)}) %collective-permute-start.41) | collective-permute-done | bytes 262176 | tf_op jit(solution)/shard_map/ppermute | solution.py:666
  355.6 23.6 %attend_back.2 = (bf16[512,384]{1,0:T(8,128)(2,1)}, bf16[512,384]{1,0:T(8,128)(2,1)}, bf16[512,384]{1,0:T(8,128)(2,1)}, bf16[512,384]{1,0:T(8,128)(2,1)}) custom-call(s32[2]{0:T(128)} %pad_add_fusion.1.place_ref, s32[1,2048]{1,0:T(1,128)} %reshape_reshape_reshape.2.start_ref, bf16[512,384]{1,0:T(8,128)(2,1)} %get-tuple-element.185.refs_0_.refs_4_.refs_8_, ...), custom_call_target="tpu_custom_call" | custom-call | flops 27599998976 | tf_op jit(solution)/shard_map/attend_back/pallas_call | solution.py:340
  379.3 24.5 %attend_back.3 = (bf16[512,384]{1,0:T(8,128)(2,1)}, bf16[512,384]{1,0:T(8,128)(2,1)}, bf16[512,384]{1,0:T(8,128)(2,1)}, bf16[512,384]{1,0:T(8,128)(2,1)}) custom-call(s32[2]{0:T(128)} %pad_add_fusion.1.place_ref, s32[1,2048]{1,0:T(1,128)} %reshape_reshape_reshape.2.start_ref, bf16[512,384]{1,0:T(8,128)(2,1)} %get-tuple-element.203.refs_0_.refs_4_.refs_8_, ...), custom_call_target="tpu_custom_call" | custom-call | flops 27599998976 | tf_op jit(solution)/shard_map/attend_back/pallas_call | solution.py:340
  410.6 13.6 %collective-permute-done.48.refs_1_ = bf16[512,384]{1,0:T(8,128)(2,1)S(1)} collective-permute-done((bf16[512,384]{1,0:T(8,128)(2,1)S(1)}, bf16[512,384]{1,0:T(8,128)(2,1)S(1)}, u32[]{:S(2)}, u32[]{:S(2)}) %collective-permute-start.48) | collective-permute-done | bytes 393248 | tf_op jit(solution)/shard_map/ppermute | solution.py:666
  433.2 8.1 %collective-permute-done.53.refs_7_ = bf16[512,384]{1,0:T(8,128)(2,1)S(1)} collective-permute-done((bf16[512,384]{1,0:T(8,128)(2,1)S(1)}, bf16[512,384]{1,0:T(8,128)(2,1)S(1)}, u32[]{:S(2)}, u32[]{:S(2)}) %collective-permute-start.53) | collective-permute-done | bytes 393248 | tf_op jit(solution)/shard_map/ppermute | solution.py:666
  442.1 19.3 %last.1 = (bf16[512,1536]{1,0:T(8,128)(2,1)}, bf16[512,1536]{1,0:T(8,128)(2,1)}, bf16[512,1536]{1,0:T(8,128)(2,1)}, bf16[512,1536]{1,0:T(8,128)(2,1)}, bf16[512,...) custom-call(s32[2]{0:T(128)} %pad_add_fusion.1.place_ref, ...), custom_call_target="tpu_custom_call" | custom-call | flops 21849999360 | tf_op jit(solution)/shard_map/last/pallas_call | solution.py:595
  484.7 15.3 %reduce-scatter.11.cloned.1.call-done = bf16[88,1024]{1,0:T(8,128)(2,1)} async-done(((bf16[352,1024]{1,0:T(8,128)(2,1)}), bf16[88,1024]{1,0:T(8,128)(2,1)}) %reduce-scatter.11.cloned.1.call-update) | async-done | bytes 180240 | tf_op jit(solution)/shard_map/reduce_scatter | solution.py:775
  503.8 10.1 %all-to-all-start.3 = ((bf16[8,96,1024]{2,1,0:T(8,128)(2,1)}), bf16[8,96,1024]{2,1,0:T(8,128)(2,1)}, u32[]{:S(2)}, u32[]{:S(2)}) async-start(bf16[8,96,1024]{2,1,0:T(8,128)(2,1)} %bitcast.152), calls=%async_computation.5 | async-start | bytes 3145728 | tf_op jit(solution)/shard_map/all_to_all | solution.py:859
  514.5 19.9 %collective-permute-done.61 = bf16[128,4224]{1,0:T(8,128)(2,1)} collective-permute-done((bf16[128,4224]{1,0:T(8,128)(2,1)}, bf16[128,4224]{1,0:T(8,128)(2,1)}, u32[]{:S(2)}, u32[]{:S(2)}) %collective-permute-start.61) | collective-permute-done | bytes 1081376 | tf_op jit(solution)/shard_map/ppermute | solution.py:644
  543.7 15.6 %collective-permute-done.62 = bf16[32,4224]{1,0:T(8,128)(2,1)S(1)} collective-permute-done((bf16[32,4224]{1,0:T(8,128)(2,1)S(1)}, bf16[32,4224]{1,0:T(8,128)(2,1)S(1)}, u32[]{:S(2)}, u32[]{:S(2)}) %collective-permute-start.62) | collective-permute-done | bytes 270368 | tf_op jit(solution)/shard_map/ppermute | solution.py:644
  559.3 7.1 %collective-permute-done.64 = bf16[32,4224]{1,0:T(8,128)(2,1)S(1)} collective-permute-done((bf16[32,4224]{1,0:T(8,128)(2,1)S(1)}, bf16[32,4224]{1,0:T(8,128)(2,1)S(1)}, u32[]{:S(2)}, u32[]{:S(2)}) %collective-permute-start.64) | collective-permute-done | bytes 270368 | tf_op jit(solution)/shard_map/ppermute | solution.py:644
  574.3 8.0 %all-to-all-start.4 = ((f32[32,8,128]{2,1,0:T(8,128)}), f32[32,8,128]{2,1,0:T(8,128)S(1)}, u32[]{:S(2)}, u32[]{:S(2)}) async-start(f32[32,8,128]{2,1,0:T(8,128)} %broadcast_in_dim_broadcast_in_dim_broadcast_in_dim.3), calls=%async_computation.8 | async-start | bytes 262144 | tf_op jit(solution)/shard_map/all_to_all | solution.py:722
  (381 shorter events, 248.2 us)
Async XLA Ops:
  17.2 37.5 %all-to-all-start = ((bf16[8,104,1024]{2,1,0:T(8,128)(2,1)}), bf16[8,104,1024]{2,1,0:T(8,128)(2,1)S(1)}, u32[]{:S(2)}, u32[]{:S(2)}) async-start(bf16[8,104,1024]{2,1,0:T(8,128)(2,1)} %pad_maximum_fusion.3), calls=%async_computation | async-start | bytes 3407872 | tf_op jit(solution)/shard_map/all_to_all | solution.py:859
  21.1 189.8 %all-gather.2.cloned.1.call-start = ((), (), s32[]{:S(2)}) async-start(), calls=%async_computation.9 | async-start | bytes 4177920 | tf_op jit(solution)/shard_map/all_gather | solution.py:890
  51.2 38.6 %collective-permute-start.16 = (s32[1,512]{1,0:T(1,128)S(1)}, s32[1,512]{1,0:T(1,128)S(1)}, u32[]{:S(2)}, u32[]{:S(2)}) collective-permute-start(s32[1,512]{1,0:T(1,128)S(1)} %bitcast.179), channel_id=1, source_target_pairs={{2,4},{3,5},{4,2},{5,3},{10,12},{11,13},{12,10},{13,11},{18,20},{1... | collective-permute-start | bytes 6152 | tf_op jit(solution)/shard_map/ppermute | solution.py:680
  57.3 36.4 %collective-permute-start = (bf16[512,1024]{1,0:T(8,128)(2,1)}, bf16[512,1024]{1,0:T(8,128)(2,1)}, u32[]{:S(2)}, u32[]{:S(2)}) collective-permute-start(bf16[512,1024]{1,0:T(8,128)(2,1)} %fusion.11), channel_id=1, source_target_pairs={{2,4},{3,5},{4,2},{5,3},{10,12},{11,13},{12,10},{13,11},{18,20},{1... | collective-permute-start | bytes 3145736 | tf_op jit(solution)/shard_map/ppermute | solution.py:680
  96.2 39.0 %collective-permute-start.18 = (s32[1,512]{1,0:T(1,128)S(1)}, s32[1,512]{1,0:T(1,128)S(1)}, u32[]{:S(2)}, u32[]{:S(2)}) collective-permute-start(s32[1,512]{1,0:T(1,128)S(1)} %broadcast_select_fusion.8), channel_id=1, source_target_pairs={{0,1},{1,0},{2,3},{3,2},{4,5},{5,4},{6,7},{7,6},{8,9},{9,8},{10,11... | collective-permute-start | bytes 6152 | tf_op jit(solution)/shard_map/ppermute | solution.py:666
  97.6 37.6 %collective-permute-start.19 = (s32[1,512]{1,0:T(1,128)S(1)}, s32[1,512]{1,0:T(1,128)S(1)}, u32[]{:S(2)}, u32[]{:S(2)}) collective-permute-start(s32[1,512]{1,0:T(1,128)S(1)} %broadcast_select_fusion.8), channel_id=1, source_target_pairs={{0,4},{1,5},{2,6},{3,7},{4,0},{5,1},{6,2},{7,3},{8,12},{9,13},{10,... | collective-permute-start | bytes 6152 | tf_op jit(solution)/shard_map/ppermute | solution.py:666
  97.6 37.6 %collective-permute-start.20 = (s32[1,512]{1,0:T(1,128)S(1)}, s32[1,512]{1,0:T(1,128)S(1)}, u32[]{:S(2)}, u32[]{:S(2)}) collective-permute-start(s32[1,512]{1,0:T(1,128)S(1)} %broadcast_select_fusion.8), channel_id=1, source_target_pairs={{0,5},{1,4},{2,7},{3,6},{4,1},{5,0},{6,3},{7,2},{8,13},{9,12},{10,... | collective-permute-start | bytes 6152 | tf_op jit(solution)/shard_map/ppermute | solution.py:666
  102.5 35.0 %collective-permute-start.34 = (bf16[128,2816]{1,0:T(8,128)(2,1)}, bf16[128,2816]{1,0:T(8,128)(2,1)}, u32[]{:S(2)}, u32[]{:S(2)}) collective-permute-start(bf16[128,2816]{1,0:T(8,128)(2,1)} %get-tuple-element.325), channel_id=1, source_target_pairs={{0,8},{8,0},{16,24},{24,16},{1,9},{9,1},{17,25},{25,17},{2,10},{10... | collective-permute-start | bytes 2162696 | tf_op jit(solution)/shard_map/ppermute | solution.py:644
  130.6 39.5 %all-to-all-start.1 = ((bf16[8,96,1024]{2,1,0:T(8,128)(2,1)}), bf16[8,96,1024]{2,1,0:T(8,128)(2,1)}, u32[]{:S(2)}, u32[]{:S(2)}) async-start(bf16[8,96,1024]{2,1,0:T(8,128)(2,1)} %bitcast.153), calls=%async_computation.1 | async-start | bytes 3145728 | tf_op jit(solution)/shard_map/all_to_all | solution.py:859
  135.1 306.3 %reduce-scatter.5.cloned.1.call-start = ((), (), s32[]{:S(2)}) async-start(), calls=%async_computation.10 | async-start | bytes 3604480 | tf_op jit(solution)/shard_map/reduce_scatter | solution.py:771
  137.6 59.3 %collective-permute-start.25 = (bf16[512,384]{1,0:T(8,128)(2,1)}, bf16[512,384]{1,0:T(8,128)(2,1)}, u32[]{:S(2)}, u32[]{:S(2)}) collective-permute-start(bf16[512,384]{1,0:T(8,128)(2,1)} %get-tuple-element.197), channel_id=1, source_target_pairs={{0,1},{1,0},{2,3},{3,2},{4,5},{5,4},{6,7},{7,6},{8,9},{9,8},{10,11... | collective-permute-start | bytes 1179656 | tf_op jit(solution)/shard_map/ppermute | solution.py:666
  139.0 57.9 %collective-permute-start.26 = (bf16[512,384]{1,0:T(8,128)(2,1)}, bf16[512,384]{1,0:T(8,128)(2,1)}, u32[]{:S(2)}, u32[]{:S(2)}) collective-permute-start(bf16[512,384]{1,0:T(8,128)(2,1)} %get-tuple-element.198), channel_id=1, source_target_pairs={{0,4},{1,5},{2,6},{3,7},{4,0},{5,1},{6,2},{7,3},{8,12},{9,13},{10,... | collective-permute-start | bytes 1179656 | tf_op jit(solution)/shard_map/ppermute | solution.py:666
  158.2 45.8 %collective-permute-start.27 = (bf16[512,384]{1,0:T(8,128)(2,1)}, bf16[512,384]{1,0:T(8,128)(2,1)}, u32[]{:S(2)}, u32[]{:S(2)}) collective-permute-start(bf16[512,384]{1,0:T(8,128)(2,1)} %get-tuple-element.199), channel_id=1, source_target_pairs={{0,5},{1,4},{2,7},{3,6},{4,1},{5,0},{6,3},{7,2},{8,13},{9,12},{10,... | collective-permute-start | bytes 1179656 | tf_op jit(solution)/shard_map/ppermute | solution.py:666
  172.6 37.3 %collective-permute-start.17 = (bf16[512,1024]{1,0:T(8,128)(2,1)S(1)}, bf16[512,1024]{1,0:T(8,128)(2,1)S(1)}, u32[]{:S(2)}, u32[]{:S(2)}) collective-permute-start(bf16[512,1024]{1,0:T(8,128)(2,1)S(1)} %fusion.12), channel_id=1, source_target_pairs={{2,4},{3,5},{4,2},{5,3},{10,12},{11,13},{12,10},{13,11},{18,20},{1... | collective-permute-start | bytes 3145736 | tf_op jit(solution)/shard_map/ppermute | solution.py:680
  204.1 34.6 %collective-permute-start.36 = (bf16[2,128,2816]{2,1,0:T(8,128)(2,1)}, bf16[2,128,2816]{2,1,0:T(8,128)(2,1)}, u32[]{:S(2)}, u32[]{:S(2)}) collective-permute-start(bf16[2,128,2816]{2,1,0:T(8,128)(2,1)} %maximum_select_fusion.8), channel_id=1, source_target_pairs={{0,16},{8,24},{16,0},{24,8},{1,17},{9,25},{17,1},{25,9},{2,18},{10... | collective-permute-start | bytes 4325384 | tf_op jit(solution)/shard_map/ppermute | solution.py:644
  208.0 33.8 %collective-permute-start.37 = (bf16[2,128,2816]{2,1,0:T(8,128)(2,1)}, bf16[2,128,2816]{2,1,0:T(8,128)(2,1)}, u32[]{:S(2)}, u32[]{:S(2)}) collective-permute-start(bf16[2,128,2816]{2,1,0:T(8,128)(2,1)} %maximum_select_fusion.9), channel_id=1, source_target_pairs={{0,8},{8,0},{16,24},{24,16},{1,9},{9,1},{17,25},{25,17},{2,10},{10... | collective-permute-start | bytes 4325384 | tf_op jit(solution)/shard_map/ppermute | solution.py:644
  211.0 41.5 %collective-permute-start.24 = (bf16[1920,1024]{1,0:T(8,128)(2,1)}, bf16[1920,1024]{1,0:T(8,128)(2,1)}, u32[]{:S(2)}, u32[]{:S(2)}) collective-permute-start(bf16[1920,1024]{1,0:T(8,128)(2,1)} %all-gather.2.cloned.1.call-done), channel_id=1, source_target_pairs={{0,4},{4,0},{1,5},{5,1},{2,6},{6,2},{3,7},{7,3},{8,12},{12,8},{9,1... | collective-permute-start | bytes 11796488 | tf_op jit(solution)/shard_map/ppermute | solution.py:644
  329.6 147.8 %reduce-scatter.7.cloned.1.call-start = ((), (), s32[]{:S(2)}) async-start(), calls=%async_computation.11 | async-start | bytes 7208960 | tf_op jit(solution)/shard_map/reduce_scatter | solution.py:771
  354.7 54.1 %collective-permute-start.40 = (bf16[512,1024]{1,0:T(8,128)(2,1)S(1)}, bf16[512,1024]{1,0:T(8,128)(2,1)S(1)}, u32[]{:S(2)}, u32[]{:S(2)}) collective-permute-start(bf16[512,1024]{1,0:T(8,128)(2,1)S(1)} %copy-done.17), channel_id=1, source_target_pairs={{2,4},{3,5},{4,2},{5,3},{10,12},{11,13},{12,10},{13,11},{18,20},{1... | collective-permute-start | bytes 3145736 | tf_op jit(solution)/shard_map/ppermute | solution.py:680
  462.5 39.2 %all-to-all-start.2 = ((bf16[8,96,1024]{2,1,0:T(8,128)(2,1)}), bf16[8,96,1024]{2,1,0:T(8,128)(2,1)S(1)}, u32[]{:S(2)}, u32[]{:S(2)}) async-start(bf16[8,96,1024]{2,1,0:T(8,128)(2,1)} %bitcast.72), calls=%async_computation.2 | async-start | bytes 3145728 | tf_op jit(solution)/shard_map/all_to_all | solution.py:859
  466.4 35.2 %collective-permute-start.58 = (bf16[512,1024]{1,0:T(8,128)(2,1)}, bf16[512,1024]{1,0:T(8,128)(2,1)}, u32[]{:S(2)}, u32[]{:S(2)}) collective-permute-start(bf16[512,1024]{1,0:T(8,128)(2,1)} %get-tuple-element.287), channel_id=1, source_target_pairs={{2,4},{3,5},{4,2},{5,3},{10,12},{11,13},{12,10},{13,11},{18,20},{1... | collective-permute-start | bytes 3145736 | tf_op jit(solution)/shard_map/ppermute | solution.py:680
  484.4 50.0 %collective-permute-start.61 = (bf16[128,4224]{1,0:T(8,128)(2,1)}, bf16[128,4224]{1,0:T(8,128)(2,1)}, u32[]{:S(2)}, u32[]{:S(2)}) collective-permute-start(bf16[128,4224]{1,0:T(8,128)(2,1)} %get-tuple-element.313), channel_id=1, source_target_pairs={{0,24},{8,16},{16,8},{24,0},{1,25},{9,17},{17,9},{25,1},{2,26},{10... | collective-permute-start | bytes 3244040 | tf_op jit(solution)/shard_map/ppermute | solution.py:644
  503.8 69.8 %all-to-all-start.3 = ((bf16[8,96,1024]{2,1,0:T(8,128)(2,1)}), bf16[8,96,1024]{2,1,0:T(8,128)(2,1)}, u32[]{:S(2)}, u32[]{:S(2)}) async-start(bf16[8,96,1024]{2,1,0:T(8,128)(2,1)} %bitcast.152), calls=%async_computation.5 | async-start | bytes 3145728 | tf_op jit(solution)/shard_map/all_to_all | solution.py:859
  513.9 56.1 %reduce-scatter.9.cloned.1.call-start = ((), (), s32[]{:S(2)}) async-start(), calls=%async_computation.12 | async-start | bytes 1802240 | tf_op jit(solution)/shard_map/reduce_scatter | solution.py:775
  (119 other events, 1434.3 us)
Sparse Core Ops, SparseCore 0:
  89.9 104.4 all-gather.1
  329.7 41.5 reduce-scatter.4
  374.2 65.8 reduce-scatter.6
  469.2 30.7 reduce-scatter.10
  516.7 42.9 reduce-scatter.8
where the time goes:
time: 611 us; the launch traced here: 606 us
  waiting for transfers between devices  196 us (32%)
  Pallas kernels  163 us (27%)
  starting transfers between devices  94.7 us (15%)
  other arithmetic  83.7 us (14%)
  local copies, waits for them, and re-layouts  25.9 us (4%)
  matrix products  22.3 us (4%)
  between operations  20.3 us (3%)
    ppermute x36, waiting for transfers between devices, swap(): return lax.ppermute(values, axis, [(i, i ^ step) for i in range(count)])  101 us
    ppermute x24, waiting for transfers between devices, group_swap(): return lax.ppermute(values, ('core', 'seq'), pairs)  73.3 us
    pallas_call x1, Pallas kernels, middle(): pl.pallas_call(functools.partial(middle_kernel, spans, width // owners),...  48.9 us
    pallas_call x2, Pallas kernels, attend_back(): pl.pallas_call(functools.partial(attend_back_kernel, spans), grid_spec=pl...  48.2 us
    ppermute x36, starting transfers between devices, swap(): return lax.ppermute(values, axis, [(i, i ^ step) for i in range(count)])  39.7 us
    pallas_call x2, Pallas kernels, attend(): pl.pallas_call(functools.partial(attend_kernel, spans), grid_spec=pltpu.P...  31.2 us
    select_n x13, other arithmetic, ordered(): jnp.where(own_bit == 0, jnp.stack([mine, other], at), jnp.stack([other, m...  28.8 us
    all_to_all x4, starting transfers between devices, exchange(): lax.all_to_all(values, ('chip', 'core'), split_axis=0, concat_axis=0, til...  22.3 us
  transfers between devices with their start and end apart: 75, of which 29 were waited for; matrix products, arithmetic and copies ran while one was open for 19% of the time, Pallas kernels for 19%

commit v1 on v0

--- a/solution.py
+++ b/solution.py
@@ -912,16 +912,17 @@
         rest = rest.reshape(-1, straight.shape[0], width)
         return [rest[:, :own_rows].reshape(-1, width), rest[:, own_rows:].reshape(-1, width)]
 
-    forward = [attend(spot, after(qkv[0], upstream), starts)]
+    positions = jnp.arange(group, dtype=jnp.int32) - starts
+    cosine_all, sine_all = rope_tables(positions.astype(F32))
+    forward = [attend(spot, after(qkv[0], upstream, cosine_all, sine_all), starts)]
     upstream = regroup(upstream)
-    positions = jnp.arange(group, dtype=jnp.int32) - after(starts, forward[0])
-    cosine_all, sine_all = rope_tables(positions.astype(F32))
     side_rest = after(side_rest, forward[0])
     other_rest = swap(side_rest, "core", 1)
     side_rest = cut_rest(side_rest)
     for pieces in cuts[1:]:
-        qkv.append(trade(pieces, forward[0]))
-        forward.append(attend(spot, after(qkv[-1], upstream, side_rest), starts))
+        qkv.append(trade(after(pieces, qkv[0]), forward[0]))
+        ready = after(qkv[-1], upstream, side_rest)
+        forward.append(attend(spot, ready, starts))
     side_gate = gather_chips(line_gate_late, came=(normed_one, forward[-1]))
     other_rest = cut_rest(after(other_rest, forward[-1]))
     weight_out = (side_rest[0], other_rest[0])
@@ -951,14 +952,15 @@
     )
     gate_kept, gate_sent, down_grad, grad_cut = rest[:2], rest[2:4], rest[4:6], rest[6:]
     grad_heads = trade(grad_cut)
-    gate_both = core_sum(gate_kept, gate_sent, grad_heads)
-    down_both = core_sum(*zip(*(row_parts(half) for half in down_grad)), grad_heads)
+    grads = [attend_back(spot, 0, qkv[0], starts, grad_heads, *forward[0][spans:], cosine_all, sine_all)]
+    gate_both = core_sum(gate_kept, gate_sent, grads[0])
+    down_both = core_sum(*zip(*(row_parts(half) for half in down_grad)), grads[0])
     grad_heads = after(grad_heads, gate_both, down_both)
     down_line = chips_scatter(down_both)
     gate_line = chips_scatter(gate_both)
-    grads = [
+    grads += [
         attend_back(spot, p, qkv[p], starts, grad_heads, *forward[p][spans:], cosine_all, sine_all)
-        for p in range(pairs)
+        for p in range(1, pairs)
     ]
     result_slots = place(anchor_slot, after(regroup(result_low, grads[0]), grads[-1]), slots)
     outputs = exchange(result_slots)
@@ -978,7 +980,7 @@
         gain_two_grad,
         normed_one,
         weight_in,
-        joined(trade(pieces) for pieces in grads),
+        joined(trade(pieces, grads[-1]) for pieces in grads),
     )
     gate_shard = line_scatter(gate_line)
     down_shard = line_scatter(after(down_line, gate_shard))
@@ -998,7 +1000,7 @@
         precision=lax.Precision.HIGHEST,
         preferred_element_type=F32,
     )
-    returned = exchange(place(anchor_slot, regroup(input_low, in_both), slots))
+    returned = exchange(place(anchor_slot, regroup(input_low, in_line), slots))
     input_gradient = pick(target_slot, returned)
     local_total = (
         jnp.sum(in_shard * in_shard)

time: 611 us -> 597 us (0.977)
  waiting for transfers between devices: 196 us -> 168 us
  starting transfers between devices: 94.7 us -> 106 us
    ppermute x24, waiting for transfers between devices: 73.3 us -> 33.2 us  [group_swap(): return lax.ppermute(values, ('core', 'seq'), pairs)]
    ppermute x24, starting transfers between devices: 18.1 us -> 41.9 us  [group_swap(): return lax.ppermute(values, ('core', 'seq'), pairs)]
    all_to_all x4, waiting for transfers between devices: 1.04 us -> 13.4 us  [exchange(): lax.all_to_all(values, ('chip', 'core'), split_axis=0, concat_axis=0, til...]
    reduce_scatter x2, waiting for transfers between devices: 15.3 us -> 4.45 us  [line_scatter(): lax.psum_scatter(values, 'seq', scatter_dimension=0, tiled=True).astype(F32)]
    ppermute x36, waiting for transfers between devices: 101 us -> 111 us  [swap(): return lax.ppermute(values, axis, [(i, i ^ step) for i in range(count)])]
    all_to_all x4, starting transfers between devices: 22.3 us -> 16.1 us  [exchange(): lax.all_to_all(values, ('chip', 'core'), split_axis=0, concat_axis=0, til...]
  transfers between devices with their start and end apart: 75 -> 75, of which waited for: 29 -> 30; matrix products, arithmetic and copies ran while one was open for 19% -> 20% of each run, Pallas kernels for 19% -> 19%
where the time goes in v1:
time: 597 us; the launch traced here: 591 us
  waiting for transfers between devices  168 us (28%)
  Pallas kernels  161 us (27%)
  starting transfers between devices  106 us (18%)
  other arithmetic  82.3 us (14%)
  local copies, waits for them, and re-layouts  27.7 us (5%)
  matrix products  24.7 us (4%)
  between operations  20.5 us (3%)
    ppermute x36, waiting for transfers between devices, swap(): return lax.ppermute(values, axis, [(i, i ^ step) for i in range(count)])  111 us
    pallas_call x1, Pallas kernels, middle(): pl.pallas_call(functools.partial(middle_kernel, spans, width // owners),...  48.4 us
    pallas_call x2, Pallas kernels, attend_back(): pl.pallas_call(functools.partial(attend_back_kernel, spans), grid_spec=pl...  47.6 us
    ppermute x24, starting transfers between devices, group_swap(): return lax.ppermute(values, ('core', 'seq'), pairs)  41.9 us
    ppermute x36, starting transfers between devices, swap(): return lax.ppermute(values, axis, [(i, i ^ step) for i in range(count)])  39.3 us
    ppermute x24, waiting for transfers between devices, group_swap(): return lax.ppermute(values, ('core', 'seq'), pairs)  33.2 us
    pallas_call x2, Pallas kernels, attend(): pl.pallas_call(functools.partial(attend_kernel, spans), grid_spec=pltpu.P...  31.2 us
    select_n x13, other arithmetic, ordered(): jnp.where(own_bit == 0, jnp.stack([mine, other], at), jnp.stack([other, m...  26.2 us
  transfers between devices with their start and end apart: 75, of which 30 were waited for; matrix products, arithmetic and copies ran while one was open for 20% of the time, Pallas kernels for 19%

profile of v1, /device:TPU:0, one launch (start us, length us, event | category | flops | bytes accessed | tf_op | source)
XLA Modules:
  0.0 591.0 jit_solution(16545392127890982109)
XLA Ops:
  21.2 7.4 %collective-permute-done.2 = bf16[32,3072]{1,0:T(8,128)(2,1)S(1)} collective-permute-done((bf16[32,3072]{1,0:T(8,128)(2,1)S(1)}, bf16[32,3072]{1,0:T(8,128)(2,1)S(1)}, u32[]{:S(2)}, u32[]{:S(2)}) %collective-permute-start.2) | collective-permute-done | bytes 196640 | tf_op jit(solution)/shard_map/ppermute | solution.py:644
  41.1 10.1 %collective-permute-done.5 = bf16[128,1536]{1,0:T(8,128)(2,1)} collective-permute-done((bf16[128,1536]{1,0:T(8,128)(2,1)}, bf16[128,1536]{1,0:T(8,128)(2,1)}, u32[]{:S(2)}, u32[]{:S(2)}) %collective-permute-start.5) | collective-permute-done | bytes 393248 | tf_op jit(solution)/shard_map/ppermute | solution.py:644
  67.4 9.1 %collective-permute-done.7 = bf16[2,128,1536]{2,1,0:T(8,128)(2,1)S(1)} collective-permute-done((bf16[2,128,1536]{2,1,0:T(8,128)(2,1)S(1)}, bf16[2,128,1536]{2,1,0:T(8,128)(2,1)S(1)}, u32[]{:S(2)}, u32[]{:S(2)}) %collective-permute-start.7) | collective-permute-done | bytes 786464 | tf_op jit(solution)/shard_map/ppermute | solution.py:644
  76.8 7.3 %collective-permute-done.6 = bf16[2,128,1536]{2,1,0:T(8,128)(2,1)S(1)} collective-permute-done((bf16[2,128,1536]{2,1,0:T(8,128)(2,1)S(1)}, bf16[2,128,1536]{2,1,0:T(8,128)(2,1)S(1)}, u32[]{:S(2)}, u32[]{:S(2)}) %collective-permute-start.6) | collective-permute-done | bytes 786464 | tf_op jit(solution)/shard_map/ppermute | solution.py:644
  113.9 15.1 %project.1 = (bf16[512,1024]{1,0:T(8,128)(2,1)}, bf16[512,384]{1,0:T(8,128)(2,1)}, bf16[512,384]{1,0:T(8,128)(2,1)}, bf16[512,384]{1,0:T(8,128)(2,1)}, bf16[512,...) custom-call(s32[2]{0:T(128)} %pad_add_fusion.1.place_ref, ...), custom_call_target="tpu_custom_call" | custom-call | flops 17250000896 | tf_op jit(solution)/shard_map/project/pallas_call | solution.py:119
  154.1 8.2 %collective-permute-done.23.refs_3_.refs_7_.refs_11_ = bf16[512,384]{1,0:T(8,128)(2,1)} collective-permute-done((bf16[512,384]{1,0:T(8,128)(2,1)}, bf16[512,384]{1,0:T(8,128)(2,1)}, u32[]{:S(2)}, u32[]{:S(2)}) %collective-permute-start.23) | collective-permute-done | bytes 393248 | tf_op jit(solution)/shard_map/ppermute | solution.py:666
  164.5 9.8 %all-to-all-done.1 = bf16[8,96,1024]{2,1,0:T(8,128)(2,1)} async-done(((bf16[8,96,1024]{2,1,0:T(8,128)(2,1)}), bf16[8,96,1024]{2,1,0:T(8,128)(2,1)}, u32[]{:S(2)}, u32[]{:S(2)}) %all-to-all-start.1) | async-done | bytes 1572896 | tf_op jit(solution)/shard_map/all_to_all | solution.py:859
  178.0 15.6 %attend.2 = (bf16[512,128]{1,0:T(8,128)(2,1)}, bf16[512,128]{1,0:T(8,128)(2,1)}, bf16[512,128]{1,0:T(8,128)(2,1)}, bf16[512,128]{1,0:T(8,128)(2,1)}, f32[4,512,128]{2,1,0:T(8,128)}, /*index=5*/f32[8,2048]{1,0:T(8,128)}) custom-call(s32[2]{0:T(128)} %pad_add_fusion.1.place_ref, s32[1,2048]{1,0:T(1,128)} %reshape_reshape_reshape.2.start_ref, ...), custom_call_target="tpu_custom_call" | custom-call | flops 18400000000 | tf_op jit(solution)/shard_map/attend/pallas_call | solution.py:225
  211.4 15.6 %attend.3 = (bf16[512,128]{1,0:T(8,128)(2,1)}, bf16[512,128]{1,0:T(8,128)(2,1)}, bf16[512,128]{1,0:T(8,128)(2,1)}, bf16[512,128]{1,0:T(8,128)(2,1)}, f32[4,512,128]{2,1,0:T(8,128)}, /*index=5*/f32[8,2048]{1,0:T(8,128)}) custom-call(s32[2]{0:T(128)} %pad_add_fusion.1.place_ref, s32[1,2048]{1,0:T(1,128)} %reshape_reshape_reshape.2.start_ref, ...), custom_call_target="tpu_custom_call" | custom-call | flops 18400000000 | tf_op jit(solution)/shard_map/attend/pallas_call | solution.py:225
  229.0 7.7 %collective-permute-done.37 = bf16[2,128,2816]{2,1,0:T(8,128)(2,1)} collective-permute-done((bf16[2,128,2816]{2,1,0:T(8,128)(2,1)}, bf16[2,128,2816]{2,1,0:T(8,128)(2,1)}, u32[]{:S(2)}, u32[]{:S(2)}) %collective-permute-start.37) | collective-permute-done | bytes 1441824 | tf_op jit(solution)/shard_map/ppermute | solution.py:644
  258.8 48.4 %middle.1 = (bf16[512,1024]{1,0:T(8,128)(2,1)}, f32[512,1024]{1,0:T(8,128)}, bf16[512,1024]{1,0:T(8,128)(2,1)}, bf16[512,512]{1,0:T(8,128)(2,1)}, bf16[512,512]{...) custom-call(s32[2]{0:T(128)} %pad_add_fusion.1.place_ref, ...), custom_call_target="tpu_custom_call" | custom-call | flops 55199997952 | tf_op jit(solution)/shard_map/middle/pallas_call | solution.py:483
  313.1 5.5 collective-permute-done.41.refs_13_
  318.7 4.7 collective-permute-done.43.refs_15_
  324.1 23.8 %attend_back.2 = (bf16[512,384]{1,0:T(8,128)(2,1)}, bf16[512,384]{1,0:T(8,128)(2,1)}, bf16[512,384]{1,0:T(8,128)(2,1)}, bf16[512,384]{1,0:T(8,128)(2,1)}) custom-call(s32[2]{0:T(128)} %pad_add_fusion.1.place_ref, s32[1,2048]{1,0:T(1,128)} %reshape_reshape_reshape.2.start_ref, bf16[512,384]{1,0:T(8,128)(2,1)} %get-tuple-element.188.refs_0_.refs_4_.refs_8_, ...), custom_call_target="tpu_custom_call" | custom-call | flops 27599998976 | tf_op jit(solution)/shard_map/attend_back/pallas_call | solution.py:340
  351.5 5.0 collective-permute-done.44
  372.1 23.8 %attend_back.3 = (bf16[512,384]{1,0:T(8,128)(2,1)}, bf16[512,384]{1,0:T(8,128)(2,1)}, bf16[512,384]{1,0:T(8,128)(2,1)}, bf16[512,384]{1,0:T(8,128)(2,1)}) custom-call(s32[2]{0:T(128)} %pad_add_fusion.1.place_ref, s32[1,2048]{1,0:T(1,128)} %reshape_reshape_reshape.2.start_ref, bf16[512,384]{1,0:T(8,128)(2,1)} %get-tuple-element.210.refs_0_.refs_4_.refs_8_, ...), custom_call_target="tpu_custom_call" | custom-call | flops 27599998976 | tf_op jit(solution)/shard_map/attend_back/pallas_call | solution.py:340
  396.8 24.1 %collective-permute-start.52 = (bf16[512,384]{1,0:T(8,128)(2,1)}, bf16[512,384]{1,0:T(8,128)(2,1)S(1)}, u32[]{:S(2)}, u32[]{:S(2)}) collective-permute-start(bf16[512,384]{1,0:T(8,128)(2,1)} %get-tuple-element.263), channel_id=1, source_target_pairs={{0,4},{1,5},{2,6},{3,7},{4,0},{5,1},{6,2},{7,3},{8,12},{9,13},{10,... | collective-permute-start | bytes 1179656 | tf_op jit(solution)/shard_map/ppermute | solution.py:666
  427.9 8.4 %collective-permute-done.53.refs_7_ = bf16[512,384]{1,0:T(8,128)(2,1)S(1)} collective-permute-done((bf16[512,384]{1,0:T(8,128)(2,1)S(1)}, bf16[512,384]{1,0:T(8,128)(2,1)S(1)}, u32[]{:S(2)}, u32[]{:S(2)}) %collective-permute-start.53) | collective-permute-done | bytes 393248 | tf_op jit(solution)/shard_map/ppermute | solution.py:666
  437.0 19.1 %last.1 = (bf16[512,1536]{1,0:T(8,128)(2,1)}, bf16[512,1536]{1,0:T(8,128)(2,1)}, bf16[512,1536]{1,0:T(8,128)(2,1)}, bf16[512,1536]{1,0:T(8,128)(2,1)}, bf16[512,...) custom-call(s32[2]{0:T(128)} %pad_add_fusion.1.place_ref, ...), custom_call_target="tpu_custom_call" | custom-call | flops 21849999360 | tf_op jit(solution)/shard_map/last/pallas_call | solution.py:595
  481.3 4.4 reduce-scatter.11.cloned.1.call-done
  489.4 15.2 %collective-permute-done.59 = bf16[128,4224]{1,0:T(8,128)(2,1)} collective-permute-done((bf16[128,4224]{1,0:T(8,128)(2,1)}, bf16[128,4224]{1,0:T(8,128)(2,1)}, u32[]{:S(2)}, u32[]{:S(2)}) %collective-permute-start.59) | collective-permute-done | bytes 1081376 | tf_op jit(solution)/shard_map/ppermute | solution.py:644
  505.5 22.7 %collective-permute-done.61 = bf16[128,4224]{1,0:T(8,128)(2,1)} collective-permute-done((bf16[128,4224]{1,0:T(8,128)(2,1)}, bf16[128,4224]{1,0:T(8,128)(2,1)}, u32[]{:S(2)}, u32[]{:S(2)}) %collective-permute-start.61) | collective-permute-done | bytes 1081376 | tf_op jit(solution)/shard_map/ppermute | solution.py:644
  543.6 9.8 %collective-permute-done.63 = bf16[32,4224]{1,0:T(8,128)(2,1)S(1)} collective-permute-done((bf16[32,4224]{1,0:T(8,128)(2,1)S(1)}, bf16[32,4224]{1,0:T(8,128)(2,1)S(1)}, u32[]{:S(2)}, u32[]{:S(2)}) %collective-permute-start.63) | collective-permute-done | bytes 270368 | tf_op jit(solution)/shard_map/ppermute | solution.py:644
  571.0 4.8 all-to-all-done.4
  (383 shorter events, 244.9 us)
Async XLA Ops:
  17.2 37.4 %all-to-all-start = ((bf16[8,104,1024]{2,1,0:T(8,128)(2,1)}), bf16[8,104,1024]{2,1,0:T(8,128)(2,1)S(1)}, u32[]{:S(2)}, u32[]{:S(2)}) async-start(bf16[8,104,1024]{2,1,0:T(8,128)(2,1)} %pad_maximum_fusion.3), calls=%async_computation | async-start | bytes 3407872 | tf_op jit(solution)/shard_map/all_to_all | solution.py:859
  21.1 186.9 %all-gather.2.cloned.1.call-start = ((), (), s32[]{:S(2)}) async-start(), calls=%async_computation.9 | async-start | bytes 4177920 | tf_op jit(solution)/shard_map/all_gather | solution.py:890
  51.1 39.6 %collective-permute-start.16 = (s32[1,512]{1,0:T(1,128)S(1)}, s32[1,512]{1,0:T(1,128)S(1)}, u32[]{:S(2)}, u32[]{:S(2)}) collective-permute-start(s32[1,512]{1,0:T(1,128)S(1)} %bitcast.182), channel_id=1, source_target_pairs={{2,4},{3,5},{4,2},{5,3},{10,12},{11,13},{12,10},{13,11},{18,20},{1... | collective-permute-start | bytes 6152 | tf_op jit(solution)/shard_map/ppermute | solution.py:680
  57.3 38.3 %collective-permute-start = (bf16[512,1024]{1,0:T(8,128)(2,1)}, bf16[512,1024]{1,0:T(8,128)(2,1)}, u32[]{:S(2)}, u32[]{:S(2)}) collective-permute-start(bf16[512,1024]{1,0:T(8,128)(2,1)} %fusion.11), channel_id=1, source_target_pairs={{2,4},{3,5},{4,2},{5,3},{10,12},{11,13},{12,10},{13,11},{18,20},{1... | collective-permute-start | bytes 3145736 | tf_op jit(solution)/shard_map/ppermute | solution.py:680
  104.3 35.2 %collective-permute-start.34 = (bf16[128,2816]{1,0:T(8,128)(2,1)}, bf16[128,2816]{1,0:T(8,128)(2,1)S(1)}, u32[]{:S(2)}, u32[]{:S(2)}) collective-permute-start(bf16[128,2816]{1,0:T(8,128)(2,1)} %get-tuple-element.331), channel_id=1, source_target_pairs={{0,8},{8,0},{16,24},{24,16},{1,9},{9,1},{17,25},{25,17},{2,10},{10... | collective-permute-start | bytes 2162696 | tf_op jit(solution)/shard_map/ppermute | solution.py:644
  129.3 33.1 %collective-permute-start.23 = (bf16[512,384]{1,0:T(8,128)(2,1)}, bf16[512,384]{1,0:T(8,128)(2,1)}, u32[]{:S(2)}, u32[]{:S(2)}) collective-permute-start(bf16[512,384]{1,0:T(8,128)(2,1)} %get-tuple-element.184), channel_id=1, source_target_pairs={{0,5},{1,4},{2,7},{3,6},{4,1},{5,0},{6,3},{7,2},{8,13},{9,12},{10,... | collective-permute-start | bytes 1179656 | tf_op jit(solution)/shard_map/ppermute | solution.py:666
  134.9 39.3 %all-to-all-start.1 = ((bf16[8,96,1024]{2,1,0:T(8,128)(2,1)}), bf16[8,96,1024]{2,1,0:T(8,128)(2,1)}, u32[]{:S(2)}, u32[]{:S(2)}) async-start(bf16[8,96,1024]{2,1,0:T(8,128)(2,1)} %bitcast.156), calls=%async_computation.1 | async-start | bytes 3145728 | tf_op jit(solution)/shard_map/all_to_all | solution.py:859
  139.2 297.0 %reduce-scatter.5.cloned.1.call-start = ((), (), s32[]{:S(2)}) async-start(), calls=%async_computation.10 | async-start | bytes 3604480 | tf_op jit(solution)/shard_map/reduce_scatter | solution.py:771
  162.3 31.4 %collective-permute-start.25 = (bf16[512,384]{1,0:T(8,128)(2,1)}, bf16[512,384]{1,0:T(8,128)(2,1)}, u32[]{:S(2)}, u32[]{:S(2)}) collective-permute-start(bf16[512,384]{1,0:T(8,128)(2,1)} %get-tuple-element.204), channel_id=1, source_target_pairs={{0,1},{1,0},{2,3},{3,2},{4,5},{5,4},{6,7},{7,6},{8,9},{9,8},{10,11... | collective-permute-start | bytes 1179656 | tf_op jit(solution)/shard_map/ppermute | solution.py:666
  162.3 33.2 %collective-permute-start.26 = (bf16[512,384]{1,0:T(8,128)(2,1)}, bf16[512,384]{1,0:T(8,128)(2,1)}, u32[]{:S(2)}, u32[]{:S(2)}) collective-permute-start(bf16[512,384]{1,0:T(8,128)(2,1)} %get-tuple-element.205), channel_id=1, source_target_pairs={{0,4},{1,5},{2,6},{3,7},{4,0},{5,1},{6,2},{7,3},{8,12},{9,13},{10,... | collective-permute-start | bytes 1179656 | tf_op jit(solution)/shard_map/ppermute | solution.py:666
  162.4 38.9 %collective-permute-start.27 = (bf16[512,384]{1,0:T(8,128)(2,1)}, bf16[512,384]{1,0:T(8,128)(2,1)}, u32[]{:S(2)}, u32[]{:S(2)}) collective-permute-start(bf16[512,384]{1,0:T(8,128)(2,1)} %get-tuple-element.206), channel_id=1, source_target_pairs={{0,5},{1,4},{2,7},{3,6},{4,1},{5,0},{6,3},{7,2},{8,13},{9,12},{10,... | collective-permute-start | bytes 1179656 | tf_op jit(solution)/shard_map/ppermute | solution.py:666
  201.4 35.4 %collective-permute-start.37 = (bf16[2,128,2816]{2,1,0:T(8,128)(2,1)}, bf16[2,128,2816]{2,1,0:T(8,128)(2,1)}, u32[]{:S(2)}, u32[]{:S(2)}) collective-permute-start(bf16[2,128,2816]{2,1,0:T(8,128)(2,1)} %maximum_select_fusion.9), channel_id=1, source_target_pairs={{0,8},{8,0},{16,24},{24,16},{1,9},{9,1},{17,25},{25,17},{2,10},{10... | collective-permute-start | bytes 4325384 | tf_op jit(solution)/shard_map/ppermute | solution.py:644
  205.8 34.0 %collective-permute-start.36 = (bf16[2,128,2816]{2,1,0:T(8,128)(2,1)}, bf16[2,128,2816]{2,1,0:T(8,128)(2,1)}, u32[]{:S(2)}, u32[]{:S(2)}) collective-permute-start(bf16[2,128,2816]{2,1,0:T(8,128)(2,1)} %maximum_select_fusion.8), channel_id=1, source_target_pairs={{0,16},{8,24},{16,0},{24,8},{1,17},{9,25},{17,1},{25,9},{2,18},{10... | collective-permute-start | bytes 4325384 | tf_op jit(solution)/shard_map/ppermute | solution.py:644
  208.0 42.4 %collective-permute-start.24 = (bf16[1920,1024]{1,0:T(8,128)(2,1)}, bf16[1920,1024]{1,0:T(8,128)(2,1)}, u32[]{:S(2)}, u32[]{:S(2)}) collective-permute-start(bf16[1920,1024]{1,0:T(8,128)(2,1)} %all-gather.2.cloned.1.call-done), channel_id=1, source_target_pairs={{0,4},{4,0},{1,5},{5,1},{2,6},{6,2},{3,7},{7,3},{8,12},{12,8},{9,1... | collective-permute-start | bytes 11796488 | tf_op jit(solution)/shard_map/ppermute | solution.py:644
  309.4 38.5 %collective-permute-start.46 = (bf16[1408,512]{1,0:T(8,128)(2,1)S(1)}, bf16[1408,512]{1,0:T(8,128)(2,1)S(1)}, u32[]{:S(2)}, u32[]{:S(2)}) collective-permute-start(bf16[1408,512]{1,0:T(8,128)(2,1)S(1)} %bitcast.160), channel_id=1, source_target_pairs={{0,4},{4,0},{1,5},{5,1},{2,6},{6,2},{3,7},{7,3},{8,12},{12,8},{9,1... | collective-permute-start | bytes 4325384 | tf_op jit(solution)/shard_map/ppermute | solution.py:644
  313.0 34.9 %collective-permute-start.47 = (bf16[1408,512]{1,0:T(8,128)(2,1)}, bf16[1408,512]{1,0:T(8,128)(2,1)S(1)}, u32[]{:S(2)}, u32[]{:S(2)}) collective-permute-start(bf16[1408,512]{1,0:T(8,128)(2,1)} %bitcast.70), channel_id=1, source_target_pairs={{0,4},{4,0},{1,5},{5,1},{2,6},{6,2},{3,7},{7,3},{8,12},{12,8},{9,1... | collective-permute-start | bytes 4325384 | tf_op jit(solution)/shard_map/ppermute | solution.py:644
  350.9 121.6 %reduce-scatter.7.cloned.1.call-start = ((), (), s32[]{:S(2)}) async-start(), calls=%async_computation.11 | async-start | bytes 7208960 | tf_op jit(solution)/shard_map/reduce_scatter | solution.py:771
  369.2 53.4 %collective-permute-start.48 = (bf16[512,384]{1,0:T(8,128)(2,1)S(1)}, bf16[512,384]{1,0:T(8,128)(2,1)S(1)}, u32[]{:S(2)}, u32[]{:S(2)}) collective-permute-start(bf16[512,384]{1,0:T(8,128)(2,1)S(1)} %copy-done.42), channel_id=1, source_target_pairs={{0,1},{1,0},{2,3},{3,2},{4,5},{5,4},{6,7},{7,6},{8,9},{9,8},{10,11... | collective-permute-start | bytes 1179656 | tf_op jit(solution)/shard_map/ppermute | solution.py:666
  369.2 56.4 %collective-permute-start.49 = (bf16[512,384]{1,0:T(8,128)(2,1)S(1)}, bf16[512,384]{1,0:T(8,128)(2,1)S(1)}, u32[]{:S(2)}, u32[]{:S(2)}) collective-permute-start(bf16[512,384]{1,0:T(8,128)(2,1)S(1)} %copy-done.41), channel_id=1, source_target_pairs={{0,4},{1,5},{2,6},{3,7},{4,0},{5,1},{6,2},{7,3},{8,12},{9,13},{10,... | collective-permute-start | bytes 1179656 | tf_op jit(solution)/shard_map/ppermute | solution.py:666
  371.0 54.7 %collective-permute-start.50 = (bf16[512,384]{1,0:T(8,128)(2,1)S(1)}, bf16[512,384]{1,0:T(8,128)(2,1)S(1)}, u32[]{:S(2)}, u32[]{:S(2)}) collective-permute-start(bf16[512,384]{1,0:T(8,128)(2,1)S(1)} %copy-done.40), channel_id=1, source_target_pairs={{0,5},{1,4},{2,7},{3,6},{4,1},{5,0},{6,3},{7,2},{8,13},{9,12},{10,... | collective-permute-start | bytes 1179656 | tf_op jit(solution)/shard_map/ppermute | solution.py:666
  395.9 31.9 %collective-permute-start.51 = (bf16[512,384]{1,0:T(8,128)(2,1)}, bf16[512,384]{1,0:T(8,128)(2,1)S(1)}, u32[]{:S(2)}, u32[]{:S(2)}) collective-permute-start(bf16[512,384]{1,0:T(8,128)(2,1)} %get-tuple-element.262), channel_id=1, source_target_pairs={{0,1},{1,0},{2,3},{3,2},{4,5},{5,4},{6,7},{7,6},{8,9},{9,8},{10,11... | collective-permute-start | bytes 1179656 | tf_op jit(solution)/shard_map/ppermute | solution.py:666
  461.4 95.5 %reduce-scatter.9.cloned.1.call-start = ((), (), s32[]{:S(2)}) async-start(), calls=%async_computation.12 | async-start | bytes 1802240 | tf_op jit(solution)/shard_map/reduce_scatter | solution.py:775
  478.5 49.7 %collective-permute-start.61 = (bf16[128,4224]{1,0:T(8,128)(2,1)}, bf16[128,4224]{1,0:T(8,128)(2,1)}, u32[]{:S(2)}, u32[]{:S(2)}) collective-permute-start(bf16[128,4224]{1,0:T(8,128)(2,1)} %get-tuple-element.319), channel_id=1, source_target_pairs={{0,24},{8,16},{16,8},{24,0},{1,25},{9,17},{17,9},{25,1},{2,26},{10... | collective-permute-start | bytes 3244040 | tf_op jit(solution)/shard_map/ppermute | solution.py:644
  479.7 55.8 %collective-permute-start.58 = (bf16[512,1024]{1,0:T(8,128)(2,1)}, bf16[512,1024]{1,0:T(8,128)(2,1)}, u32[]{:S(2)}, u32[]{:S(2)}) collective-permute-start(bf16[512,1024]{1,0:T(8,128)(2,1)} %get-tuple-element.293), channel_id=1, source_target_pairs={{2,4},{3,5},{4,2},{5,3},{10,12},{11,13},{12,10},{13,11},{18,20},{1... | collective-permute-start | bytes 3145736 | tf_op jit(solution)/shard_map/ppermute | solution.py:680
  (120 other events, 1341.4 us)
Sparse Core Ops, SparseCore 0:
  90.9 106.4 all-gather.1
  351.0 40.3 reduce-scatter.4
  394.4 65.7 reduce-scatter.6
  463.6 22.0 reduce-scatter.10
  487.9 36.0 reduce-scatter.8

commit v2 on v1

--- a/solution.py
+++ b/solution.py
@@ -81,7 +81,7 @@
 
 def project_kernel(spans, half, place_ref, x_ref, gain_ref, wa_ref, wb_ref, cos_ref, sin_ref, h_ref, *outs):
     step = pl.program_id(0)
-    hw = wa_ref.shape[1]
+    hw = wa_ref.shape[1] // 2
 
     @pl.when(step == 0)
     def _():
@@ -93,19 +93,21 @@
         acc = jnp.dot(h_ref[...], w_ref[...], preferred_element_type=F32)
         if rotated:
             pieces = []
-            for c in range(hw // LANES):
+            for c in range(2 * hw // LANES):
                 part = acc[:, c * LANES : (c + 1) * LANES]
                 pieces.append(part * cos_ref[...] + swap_halves(part) * sin_ref[...])
             acc = jnp.concatenate(pieces, axis=1)
         low = acc.astype(BF16)
-        for k in range(spans):
-
-            @pl.when((step % spans) ^ place_ref[0] == k)
-            def _(k=k):
-                for pair in range(hw // LANES):
-                    outs[pair * spans + k][...] = low[:, pair * LANES : (pair + 1) * LANES]
-
-    turning = step < 2 * spans
+        for side in range(2):
+            for k in range(spans):
+
+                @pl.when(((2 * step + side) % spans) ^ place_ref[0] == k)
+                def _(k=k, side=side):
+                    for pair in range(hw // LANES):
+                        lo = side * hw + pair * LANES
+                        outs[pair * spans + k][...] = low[:, lo : lo + LANES]
+
+    turning = step < spans
     pl.when(step < half)(lambda: work(wa_ref, True))
     pl.when((step >= half) & turning)(lambda: work(wb_ref, True))
     pl.when(jnp.logical_not(turning))(lambda: work(wb_ref, False))
@@ -114,23 +116,23 @@
 def project(spot, x, gain_row, weights, cosine, sine, spans):
     rows, width = x.shape
     hw = width // spans
-    half = 3 * spans // 2
+    half = 3 * spans // 4
     fixed = lambda t, p: (0, 0)
     return pl.pallas_call(
         functools.partial(project_kernel, spans, half),
         grid_spec=pltpu.PrefetchScalarGridSpec(
             num_scalar_prefetch=1,
-            grid=(3 * spans,),
+            grid=(3 * spans // 2,),
             in_specs=[
                 pl.BlockSpec((rows, width), fixed),
                 pl.BlockSpec((1, width), fixed),
-                pl.BlockSpec((width, hw), lambda t, p: (0, jnp.minimum(t, half - 1))),
-                pl.BlockSpec((width, hw), lambda t, p: (0, jnp.maximum(t - half, 0))),
+                pl.BlockSpec((width, 2 * hw), lambda t, p: (0, jnp.minimum(t, half - 1))),
+                pl.BlockSpec((width, 2 * hw), lambda t, p: (0, jnp.maximum(t - half, 0))),
                 pl.BlockSpec((rows, LANES), fixed),
                 pl.BlockSpec((rows, LANES), fixed),
             ],
             out_specs=[pl.BlockSpec((rows, width), fixed)]
-            + [pl.BlockSpec((rows, LANES), lambda t, p: (0, t // spans))] * (width // LANES),
+            + [pl.BlockSpec((rows, LANES), lambda t, p: (0, 2 * t // spans))] * (width // LANES),
         ),
         out_shape=[jax.ShapeDtypeStruct((rows, width), BF16)]
         + [jax.ShapeDtypeStruct((rows, 3 * LANES), BF16)] * (width // LANES),
@@ -549,12 +551,14 @@
         sent_scr[...] = sent.T.astype(BF16)
         dh_scr[...] = jnp.zeros_like(dh_scr)
 
-    for k in range(spans):
-
-        @pl.when((step % spans) ^ place_ref[0] == k)
-        def _(k=k):
-            for pair in range(heads // spans):
-                d_scr[:, pair * LANES : (pair + 1) * LANES] = pieces[pair * spans + k][...]
+    for side in range(2):
+        for k in range(spans):
+
+            @pl.when(((2 * step + side) % spans) ^ place_ref[0] == k)
+            def _(k=k, side=side):
+                for pair in range(heads // spans):
+                    lo = side * (heads // spans) * LANES + pair * LANES
+                    d_scr[:, lo : lo + LANES] = pieces[pair * spans + k][...]
 
     def work(w_ref, s_ref, k_ref):
         d = d_scr[...]
@@ -584,8 +588,8 @@
 
 def last(spot, owners, spans, x, dx2, gain_row, gain_two_grad, normed, weights, pieces):
     rows, width = x.shape
-    hw = width // spans
-    half = 3 * spans // 2
+    hw = 2 * width // spans
+    half = 3 * spans // 4
     low = lambda t, s: (0, jnp.minimum(t, half - 1))
     high = lambda t, s: (0, jnp.maximum(t - half, 0))
     fixed = lambda t, s: (0, 0)
@@ -596,10 +600,10 @@
         functools.partial(last_kernel, spans, half, width // owners),
         grid_spec=pltpu.PrefetchScalarGridSpec(
             num_scalar_prefetch=1,
-            grid=(3 * spans,),
+            grid=(3 * spans // 2,),
             in_specs=[full, full, row, row, full]
             + [pl.BlockSpec((width, hw), low), pl.BlockSpec((width, hw), high)]
-            + [pl.BlockSpec((rows, LANES), lambda t, s: (0, t // spans))] * len(pieces),
+            + [pl.BlockSpec((rows, LANES), lambda t, s: (0, 2 * t // spans))] * len(pieces),
             out_specs=[
                 pl.BlockSpec((width // 2, hw), low),
                 pl.BlockSpec((width // 2, hw), high),

time: 597 us -> 592 us (level)
  no operation moved by 1% of the time
where the time goes in v2:
time: 592 us; the launch traced here: 587 us
  waiting for transfers between devices  169 us (29%)
  Pallas kernels  157 us (27%)
  starting transfers between devices  105 us (18%)
  other arithmetic  81.9 us (14%)
  local copies, waits for them, and re-layouts  27.6 us (5%)
  matrix products  24.7 us (4%)
  between operations  20.6 us (3%)
    ppermute x36, waiting for transfers between devices, swap(): return lax.ppermute(values, axis, [(i, i ^ step) for i in range(count)])  110 us
    pallas_call x1, Pallas kernels, middle(): pl.pallas_call(functools.partial(middle_kernel, spans, width // owners),...  48.4 us
    pallas_call x2, Pallas kernels, attend_back(): pl.pallas_call(functools.partial(attend_back_kernel, spans), grid_spec=pl...  47.6 us
    ppermute x24, starting transfers between devices, group_swap(): return lax.ppermute(values, ('core', 'seq'), pairs)  43 us
    ppermute x36, starting transfers between devices, swap(): return lax.ppermute(values, axis, [(i, i ^ step) for i in range(count)])  37 us
    ppermute x24, waiting for transfers between devices, group_swap(): return lax.ppermute(values, ('core', 'seq'), pairs)  36.7 us
    pallas_call x2, Pallas kernels, attend(): pl.pallas_call(functools.partial(attend_kernel, spans), grid_spec=pltpu.P...  31.2 us
    select_n x13, other arithmetic, ordered(): jnp.where(own_bit == 0, jnp.stack([mine, other], at), jnp.stack([other, m...  26.1 us
  transfers between devices with their start and end apart: 75, of which 30 were waited for; matrix products, arithmetic and copies ran while one was open for 20% of the time, Pallas kernels for 19%

profile of v2, /device:TPU:0, one launch (start us, length us, event | category | flops | bytes accessed | tf_op | source)
XLA Modules:
  0.0 586.9 jit_solution(2463016520027573676)
XLA Ops:
  21.2 7.4 %collective-permute-done.2 = bf16[32,3072]{1,0:T(8,128)(2,1)S(1)} collective-permute-done((bf16[32,3072]{1,0:T(8,128)(2,1)S(1)}, bf16[32,3072]{1,0:T(8,128)(2,1)S(1)}, u32[]{:S(2)}, u32[]{:S(2)}) %collective-permute-start.2) | collective-permute-done | bytes 196640 | tf_op jit(solution)/shard_map/ppermute | solution.py:648
  41.1 10.1 %collective-permute-done.5 = bf16[128,1536]{1,0:T(8,128)(2,1)} collective-permute-done((bf16[128,1536]{1,0:T(8,128)(2,1)}, bf16[128,1536]{1,0:T(8,128)(2,1)}, u32[]{:S(2)}, u32[]{:S(2)}) %collective-permute-start.5) | collective-permute-done | bytes 393248 | tf_op jit(solution)/shard_map/ppermute | solution.py:648
  67.4 9.1 %collective-permute-done.7 = bf16[2,128,1536]{2,1,0:T(8,128)(2,1)S(1)} collective-permute-done((bf16[2,128,1536]{2,1,0:T(8,128)(2,1)S(1)}, bf16[2,128,1536]{2,1,0:T(8,128)(2,1)S(1)}, u32[]{:S(2)}, u32[]{:S(2)}) %collective-permute-start.7) | collective-permute-done | bytes 786464 | tf_op jit(solution)/shard_map/ppermute | solution.py:648
  76.8 7.3 %collective-permute-done.6 = bf16[2,128,1536]{2,1,0:T(8,128)(2,1)S(1)} collective-permute-done((bf16[2,128,1536]{2,1,0:T(8,128)(2,1)S(1)}, bf16[2,128,1536]{2,1,0:T(8,128)(2,1)S(1)}, u32[]{:S(2)}, u32[]{:S(2)}) %collective-permute-start.6) | collective-permute-done | bytes 786464 | tf_op jit(solution)/shard_map/ppermute | solution.py:648
  113.9 12.6 %project.1 = (bf16[512,1024]{1,0:T(8,128)(2,1)}, bf16[512,384]{1,0:T(8,128)(2,1)}, bf16[512,384]{1,0:T(8,128)(2,1)}, bf16[512,384]{1,0:T(8,128)(2,1)}, bf16[512,...) custom-call(s32[2]{0:T(128)} %pad_add_fusion.1.place_ref, ...), custom_call_target="tpu_custom_call" | custom-call | flops 17250000896 | tf_op jit(solution)/shard_map/project/pallas_call | solution.py:121
  151.6 6.8 %collective-permute-done.23.refs_3_.refs_7_.refs_11_ = bf16[512,384]{1,0:T(8,128)(2,1)} collective-permute-done((bf16[512,384]{1,0:T(8,128)(2,1)}, bf16[512,384]{1,0:T(8,128)(2,1)}, u32[]{:S(2)}, u32[]{:S(2)}) %collective-permute-start.23) | collective-permute-done | bytes 393248 | tf_op jit(solution)/shard_map/ppermute | solution.py:670
  162.1 7.7 %all-to-all-done.1 = bf16[8,96,1024]{2,1,0:T(8,128)(2,1)} async-done(((bf16[8,96,1024]{2,1,0:T(8,128)(2,1)}), bf16[8,96,1024]{2,1,0:T(8,128)(2,1)}, u32[]{:S(2)}, u32[]{:S(2)}) %all-to-all-start.1) | async-done | bytes 1572896 | tf_op jit(solution)/shard_map/all_to_all | solution.py:863
  173.7 15.6 %attend.2 = (bf16[512,128]{1,0:T(8,128)(2,1)}, bf16[512,128]{1,0:T(8,128)(2,1)}, bf16[512,128]{1,0:T(8,128)(2,1)}, bf16[512,128]{1,0:T(8,128)(2,1)}, f32[4,512,128]{2,1,0:T(8,128)}, /*index=5*/f32[8,2048]{1,0:T(8,128)}) custom-call(s32[2]{0:T(128)} %pad_add_fusion.1.place_ref, s32[1,2048]{1,0:T(1,128)} %reshape_reshape_reshape.2.start_ref, ...), custom_call_target="tpu_custom_call" | custom-call | flops 18400000000 | tf_op jit(solution)/shard_map/attend/pallas_call | solution.py:227
  192.8 8.2 %collective-permute-done.27.refs_3_.refs_7_.refs_11_ = bf16[512,384]{1,0:T(8,128)(2,1)} collective-permute-done((bf16[512,384]{1,0:T(8,128)(2,1)}, bf16[512,384]{1,0:T(8,128)(2,1)}, u32[]{:S(2)}, u32[]{:S(2)}) %collective-permute-start.27) | collective-permute-done | bytes 393248 | tf_op jit(solution)/shard_map/ppermute | solution.py:670
  209.8 15.6 %attend.3 = (bf16[512,128]{1,0:T(8,128)(2,1)}, bf16[512,128]{1,0:T(8,128)(2,1)}, bf16[512,128]{1,0:T(8,128)(2,1)}, bf16[512,128]{1,0:T(8,128)(2,1)}, f32[4,512,128]{2,1,0:T(8,128)}, /*index=5*/f32[8,2048]{1,0:T(8,128)}) custom-call(s32[2]{0:T(128)} %pad_add_fusion.1.place_ref, s32[1,2048]{1,0:T(1,128)} %reshape_reshape_reshape.2.start_ref, ...), custom_call_target="tpu_custom_call" | custom-call | flops 18400000000 | tf_op jit(solution)/shard_map/attend/pallas_call | solution.py:227
  226.6 7.8 %collective-permute-done.37 = bf16[2,128,2816]{2,1,0:T(8,128)(2,1)} collective-permute-done((bf16[2,128,2816]{2,1,0:T(8,128)(2,1)}, bf16[2,128,2816]{2,1,0:T(8,128)(2,1)}, u32[]{:S(2)}, u32[]{:S(2)}) %collective-permute-start.37) | collective-permute-done | bytes 1441824 | tf_op jit(solution)/shard_map/ppermute | solution.py:648
  256.4 48.4 %middle.1 = (bf16[512,1024]{1,0:T(8,128)(2,1)}, f32[512,1024]{1,0:T(8,128)}, bf16[512,1024]{1,0:T(8,128)(2,1)}, bf16[512,512]{1,0:T(8,128)(2,1)}, bf16[512,512]{...) custom-call(s32[2]{0:T(128)} %pad_add_fusion.1.place_ref, ...), custom_call_target="tpu_custom_call" | custom-call | flops 55199997952 | tf_op jit(solution)/shard_map/middle/pallas_call | solution.py:485
  310.7 5.5 collective-permute-done.41.refs_13_
  321.7 23.8 %attend_back.2 = (bf16[512,384]{1,0:T(8,128)(2,1)}, bf16[512,384]{1,0:T(8,128)(2,1)}, bf16[512,384]{1,0:T(8,128)(2,1)}, bf16[512,384]{1,0:T(8,128)(2,1)}) custom-call(s32[2]{0:T(128)} %pad_add_fusion.1.place_ref, s32[1,2048]{1,0:T(1,128)} %reshape_reshape_reshape.2.start_ref, bf16[512,384]{1,0:T(8,128)(2,1)} %get-tuple-element.188.refs_0_.refs_4_.refs_8_, ...), custom_call_target="tpu_custom_call" | custom-call | flops 27599998976 | tf_op jit(solution)/shard_map/attend_back/pallas_call | solution.py:342
  349.1 5.0 collective-permute-done.44
  370.6 23.8 %attend_back.3 = (bf16[512,384]{1,0:T(8,128)(2,1)}, bf16[512,384]{1,0:T(8,128)(2,1)}, bf16[512,384]{1,0:T(8,128)(2,1)}, bf16[512,384]{1,0:T(8,128)(2,1)}) custom-call(s32[2]{0:T(128)} %pad_add_fusion.1.place_ref, s32[1,2048]{1,0:T(1,128)} %reshape_reshape_reshape.2.start_ref, bf16[512,384]{1,0:T(8,128)(2,1)} %get-tuple-element.210.refs_0_.refs_4_.refs_8_, ...), custom_call_target="tpu_custom_call" | custom-call | flops 27599998976 | tf_op jit(solution)/shard_map/attend_back/pallas_call | solution.py:342
  396.0 22.5 %collective-permute-start.52 = (bf16[512,384]{1,0:T(8,128)(2,1)}, bf16[512,384]{1,0:T(8,128)(2,1)S(1)}, u32[]{:S(2)}, u32[]{:S(2)}) collective-permute-start(bf16[512,384]{1,0:T(8,128)(2,1)} %get-tuple-element.263), channel_id=1, source_target_pairs={{0,4},{1,5},{2,6},{3,7},{4,0},{5,1},{6,2},{7,3},{8,12},{9,13},{10,... | collective-permute-start | bytes 1179656 | tf_op jit(solution)/shard_map/ppermute | solution.py:670
  425.6 8.4 %collective-permute-done.53.refs_7_ = bf16[512,384]{1,0:T(8,128)(2,1)S(1)} collective-permute-done((bf16[512,384]{1,0:T(8,128)(2,1)S(1)}, bf16[512,384]{1,0:T(8,128)(2,1)S(1)}, u32[]{:S(2)}, u32[]{:S(2)}) %collective-permute-start.53) | collective-permute-done | bytes 393248 | tf_op jit(solution)/shard_map/ppermute | solution.py:670
  434.7 17.3 %last.1 = (bf16[512,1536]{1,0:T(8,128)(2,1)}, bf16[512,1536]{1,0:T(8,128)(2,1)}, bf16[512,1536]{1,0:T(8,128)(2,1)}, bf16[512,1536]{1,0:T(8,128)(2,1)}, bf16[512,...) custom-call(s32[2]{0:T(128)} %pad_add_fusion.1.place_ref, ...), custom_call_target="tpu_custom_call" | custom-call | flops 21849999360 | tf_op jit(solution)/shard_map/last/pallas_call | solution.py:599
  476.8 5.7 reduce-scatter.11.cloned.1.call-done
  486.2 14.2 %collective-permute-done.59 = bf16[128,4224]{1,0:T(8,128)(2,1)} collective-permute-done((bf16[128,4224]{1,0:T(8,128)(2,1)}, bf16[128,4224]{1,0:T(8,128)(2,1)}, u32[]{:S(2)}, u32[]{:S(2)}) %collective-permute-start.59) | collective-permute-done | bytes 1081376 | tf_op jit(solution)/shard_map/ppermute | solution.py:648
  501.3 22.8 %collective-permute-done.61 = bf16[128,4224]{1,0:T(8,128)(2,1)} collective-permute-done((bf16[128,4224]{1,0:T(8,128)(2,1)}, bf16[128,4224]{1,0:T(8,128)(2,1)}, u32[]{:S(2)}, u32[]{:S(2)}) %collective-permute-start.61) | collective-permute-done | bytes 1081376 | tf_op jit(solution)/shard_map/ppermute | solution.py:648
  539.7 9.2 %collective-permute-done.63 = bf16[32,4224]{1,0:T(8,128)(2,1)S(1)} collective-permute-done((bf16[32,4224]{1,0:T(8,128)(2,1)S(1)}, bf16[32,4224]{1,0:T(8,128)(2,1)S(1)}, u32[]{:S(2)}, u32[]{:S(2)}) %collective-permute-start.63) | collective-permute-done | bytes 270368 | tf_op jit(solution)/shard_map/ppermute | solution.py:648
  566.9 4.8 all-to-all-done.4
  (383 shorter events, 246.7 us)
Async XLA Ops:
  17.2 37.4 %all-to-all-start = ((bf16[8,104,1024]{2,1,0:T(8,128)(2,1)}), bf16[8,104,1024]{2,1,0:T(8,128)(2,1)S(1)}, u32[]{:S(2)}, u32[]{:S(2)}) async-start(bf16[8,104,1024]{2,1,0:T(8,128)(2,1)} %pad_maximum_fusion.3), calls=%async_computation | async-start | bytes 3407872 | tf_op jit(solution)/shard_map/all_to_all | solution.py:863
  21.1 186.3 %all-gather.2.cloned.1.call-start = ((), (), s32[]{:S(2)}) async-start(), calls=%async_computation.9 | async-start | bytes 4177920 | tf_op jit(solution)/shard_map/all_gather | solution.py:894
  51.1 39.6 %collective-permute-start.16 = (s32[1,512]{1,0:T(1,128)S(1)}, s32[1,512]{1,0:T(1,128)S(1)}, u32[]{:S(2)}, u32[]{:S(2)}) collective-permute-start(s32[1,512]{1,0:T(1,128)S(1)} %bitcast.182), channel_id=1, source_target_pairs={{2,4},{3,5},{4,2},{5,3},{10,12},{11,13},{12,10},{13,11},{18,20},{1... | collective-permute-start | bytes 6152 | tf_op jit(solution)/shard_map/ppermute | solution.py:684
  57.2 38.4 %collective-permute-start = (bf16[512,1024]{1,0:T(8,128)(2,1)}, bf16[512,1024]{1,0:T(8,128)(2,1)}, u32[]{:S(2)}, u32[]{:S(2)}) collective-permute-start(bf16[512,1024]{1,0:T(8,128)(2,1)} %fusion.11), channel_id=1, source_target_pairs={{2,4},{3,5},{4,2},{5,3},{10,12},{11,13},{12,10},{13,11},{18,20},{1... | collective-permute-start | bytes 3145736 | tf_op jit(solution)/shard_map/ppermute | solution.py:684
  104.3 32.8 %collective-permute-start.34 = (bf16[128,2816]{1,0:T(8,128)(2,1)}, bf16[128,2816]{1,0:T(8,128)(2,1)S(1)}, u32[]{:S(2)}, u32[]{:S(2)}) collective-permute-start(bf16[128,2816]{1,0:T(8,128)(2,1)} %get-tuple-element.331), channel_id=1, source_target_pairs={{0,8},{8,0},{16,24},{24,16},{1,9},{9,1},{17,25},{25,17},{2,10},{10... | collective-permute-start | bytes 2162696 | tf_op jit(solution)/shard_map/ppermute | solution.py:648
  126.8 31.6 %collective-permute-start.23 = (bf16[512,384]{1,0:T(8,128)(2,1)}, bf16[512,384]{1,0:T(8,128)(2,1)}, u32[]{:S(2)}, u32[]{:S(2)}) collective-permute-start(bf16[512,384]{1,0:T(8,128)(2,1)} %get-tuple-element.184), channel_id=1, source_target_pairs={{0,5},{1,4},{2,7},{3,6},{4,1},{5,0},{6,3},{7,2},{8,13},{9,12},{10,... | collective-permute-start | bytes 1179656 | tf_op jit(solution)/shard_map/ppermute | solution.py:670
  132.5 37.4 %all-to-all-start.1 = ((bf16[8,96,1024]{2,1,0:T(8,128)(2,1)}), bf16[8,96,1024]{2,1,0:T(8,128)(2,1)}, u32[]{:S(2)}, u32[]{:S(2)}) async-start(bf16[8,96,1024]{2,1,0:T(8,128)(2,1)} %bitcast.156), calls=%async_computation.1 | async-start | bytes 3145728 | tf_op jit(solution)/shard_map/all_to_all | solution.py:863
  136.8 297.2 %reduce-scatter.5.cloned.1.call-start = ((), (), s32[]{:S(2)}) async-start(), calls=%async_computation.10 | async-start | bytes 3604480 | tf_op jit(solution)/shard_map/reduce_scatter | solution.py:775
  160.8 40.3 %collective-permute-start.27 = (bf16[512,384]{1,0:T(8,128)(2,1)}, bf16[512,384]{1,0:T(8,128)(2,1)}, u32[]{:S(2)}, u32[]{:S(2)}) collective-permute-start(bf16[512,384]{1,0:T(8,128)(2,1)} %get-tuple-element.206), channel_id=1, source_target_pairs={{0,5},{1,4},{2,7},{3,6},{4,1},{5,0},{6,3},{7,2},{8,13},{9,12},{10,... | collective-permute-start | bytes 1179656 | tf_op jit(solution)/shard_map/ppermute | solution.py:670
  172.3 33.9 %collective-permute-start.17 = (bf16[512,1024]{1,0:T(8,128)(2,1)S(1)}, bf16[512,1024]{1,0:T(8,128)(2,1)S(1)}, u32[]{:S(2)}, u32[]{:S(2)}) collective-permute-start(bf16[512,1024]{1,0:T(8,128)(2,1)S(1)} %fusion.12), channel_id=1, source_target_pairs={{2,4},{3,5},{4,2},{5,3},{10,12},{11,13},{12,10},{13,11},{18,20},{1... | collective-permute-start | bytes 3145736 | tf_op jit(solution)/shard_map/ppermute | solution.py:684
  201.0 33.3 %collective-permute-start.37 = (bf16[2,128,2816]{2,1,0:T(8,128)(2,1)}, bf16[2,128,2816]{2,1,0:T(8,128)(2,1)}, u32[]{:S(2)}, u32[]{:S(2)}) collective-permute-start(bf16[2,128,2816]{2,1,0:T(8,128)(2,1)} %maximum_select_fusion.9), channel_id=1, source_target_pairs={{0,8},{8,0},{16,24},{24,16},{1,9},{9,1},{17,25},{25,17},{2,10},{10... | collective-permute-start | bytes 4325384 | tf_op jit(solution)/shard_map/ppermute | solution.py:648
  203.2 34.2 %collective-permute-start.36 = (bf16[2,128,2816]{2,1,0:T(8,128)(2,1)}, bf16[2,128,2816]{2,1,0:T(8,128)(2,1)}, u32[]{:S(2)}, u32[]{:S(2)}) collective-permute-start(bf16[2,128,2816]{2,1,0:T(8,128)(2,1)} %maximum_select_fusion.8), channel_id=1, source_target_pairs={{0,16},{8,24},{16,0},{24,8},{1,17},{9,25},{17,1},{25,9},{2,18},{10... | collective-permute-start | bytes 4325384 | tf_op jit(solution)/shard_map/ppermute | solution.py:648
  207.4 40.7 %collective-permute-start.24 = (bf16[1920,1024]{1,0:T(8,128)(2,1)}, bf16[1920,1024]{1,0:T(8,128)(2,1)}, u32[]{:S(2)}, u32[]{:S(2)}) collective-permute-start(bf16[1920,1024]{1,0:T(8,128)(2,1)} %all-gather.2.cloned.1.call-done), channel_id=1, source_target_pairs={{0,4},{4,0},{1,5},{5,1},{2,6},{6,2},{3,7},{7,3},{8,12},{12,8},{9,1... | collective-permute-start | bytes 11796488 | tf_op jit(solution)/shard_map/ppermute | solution.py:648
  307.0 38.5 %collective-permute-start.46 = (bf16[1408,512]{1,0:T(8,128)(2,1)S(1)}, bf16[1408,512]{1,0:T(8,128)(2,1)S(1)}, u32[]{:S(2)}, u32[]{:S(2)}) collective-permute-start(bf16[1408,512]{1,0:T(8,128)(2,1)S(1)} %bitcast.160), channel_id=1, source_target_pairs={{0,4},{4,0},{1,5},{5,1},{2,6},{6,2},{3,7},{7,3},{8,12},{12,8},{9,1... | collective-permute-start | bytes 4325384 | tf_op jit(solution)/shard_map/ppermute | solution.py:648
  310.6 34.9 %collective-permute-start.47 = (bf16[1408,512]{1,0:T(8,128)(2,1)}, bf16[1408,512]{1,0:T(8,128)(2,1)S(1)}, u32[]{:S(2)}, u32[]{:S(2)}) collective-permute-start(bf16[1408,512]{1,0:T(8,128)(2,1)} %bitcast.70), channel_id=1, source_target_pairs={{0,4},{4,0},{1,5},{5,1},{2,6},{6,2},{3,7},{7,3},{8,12},{12,8},{9,1... | collective-permute-start | bytes 4325384 | tf_op jit(solution)/shard_map/ppermute | solution.py:648
  348.5 119.5 %reduce-scatter.7.cloned.1.call-start = ((), (), s32[]{:S(2)}) async-start(), calls=%async_computation.11 | async-start | bytes 7208960 | tf_op jit(solution)/shard_map/reduce_scatter | solution.py:775
  366.6 53.7 %collective-permute-start.48 = (bf16[512,384]{1,0:T(8,128)(2,1)S(1)}, bf16[512,384]{1,0:T(8,128)(2,1)S(1)}, u32[]{:S(2)}, u32[]{:S(2)}) collective-permute-start(bf16[512,384]{1,0:T(8,128)(2,1)S(1)} %copy-done.42), channel_id=1, source_target_pairs={{0,1},{1,0},{2,3},{3,2},{4,5},{5,4},{6,7},{7,6},{8,9},{9,8},{10,11... | collective-permute-start | bytes 1179656 | tf_op jit(solution)/shard_map/ppermute | solution.py:670
  367.2 56.2 %collective-permute-start.49 = (bf16[512,384]{1,0:T(8,128)(2,1)S(1)}, bf16[512,384]{1,0:T(8,128)(2,1)S(1)}, u32[]{:S(2)}, u32[]{:S(2)}) collective-permute-start(bf16[512,384]{1,0:T(8,128)(2,1)S(1)} %copy-done.41), channel_id=1, source_target_pairs={{0,4},{1,5},{2,6},{3,7},{4,0},{5,1},{6,2},{7,3},{8,12},{9,13},{10,... | collective-permute-start | bytes 1179656 | tf_op jit(solution)/shard_map/ppermute | solution.py:670
  370.3 53.0 %collective-permute-start.50 = (bf16[512,384]{1,0:T(8,128)(2,1)S(1)}, bf16[512,384]{1,0:T(8,128)(2,1)S(1)}, u32[]{:S(2)}, u32[]{:S(2)}) collective-permute-start(bf16[512,384]{1,0:T(8,128)(2,1)S(1)} %copy-done.40), channel_id=1, source_target_pairs={{0,5},{1,4},{2,7},{3,6},{4,1},{5,0},{6,3},{7,2},{8,13},{9,12},{10,... | collective-permute-start | bytes 1179656 | tf_op jit(solution)/shard_map/ppermute | solution.py:670
  394.4 31.1 %collective-permute-start.51 = (bf16[512,384]{1,0:T(8,128)(2,1)}, bf16[512,384]{1,0:T(8,128)(2,1)S(1)}, u32[]{:S(2)}, u32[]{:S(2)}) collective-permute-start(bf16[512,384]{1,0:T(8,128)(2,1)} %get-tuple-element.262), channel_id=1, source_target_pairs={{0,1},{1,0},{2,3},{3,2},{4,5},{5,4},{6,7},{7,6},{8,9},{9,8},{10,11... | collective-permute-start | bytes 1179656 | tf_op jit(solution)/shard_map/ppermute | solution.py:670
  453.1 31.1 %all-to-all-start.2 = ((bf16[8,96,1024]{2,1,0:T(8,128)(2,1)}), bf16[8,96,1024]{2,1,0:T(8,128)(2,1)S(1)}, u32[]{:S(2)}, u32[]{:S(2)}) async-start(bf16[8,96,1024]{2,1,0:T(8,128)(2,1)} %bitcast.72), calls=%async_computation.2 | async-start | bytes 3145728 | tf_op jit(solution)/shard_map/all_to_all | solution.py:863
  457.2 95.2 %reduce-scatter.9.cloned.1.call-start = ((), (), s32[]{:S(2)}) async-start(), calls=%async_computation.12 | async-start | bytes 1802240 | tf_op jit(solution)/shard_map/reduce_scatter | solution.py:779
  473.6 50.5 %collective-permute-start.61 = (bf16[128,4224]{1,0:T(8,128)(2,1)}, bf16[128,4224]{1,0:T(8,128)(2,1)}, u32[]{:S(2)}, u32[]{:S(2)}) collective-permute-start(bf16[128,4224]{1,0:T(8,128)(2,1)} %get-tuple-element.319), channel_id=1, source_target_pairs={{0,24},{8,16},{16,8},{24,0},{1,25},{9,17},{17,9},{25,1},{2,26},{10... | collective-permute-start | bytes 3244040 | tf_op jit(solution)/shard_map/ppermute | solution.py:648
  475.2 56.2 %collective-permute-start.58 = (bf16[512,1024]{1,0:T(8,128)(2,1)}, bf16[512,1024]{1,0:T(8,128)(2,1)}, u32[]{:S(2)}, u32[]{:S(2)}) collective-permute-start(bf16[512,1024]{1,0:T(8,128)(2,1)} %get-tuple-element.293), channel_id=1, source_target_pairs={{2,4},{3,5},{4,2},{5,3},{10,12},{11,13},{12,10},{13,11},{18,20},{1... | collective-permute-start | bytes 3145736 | tf_op jit(solution)/shard_map/ppermute | solution.py:684
  (120 other events, 1342.4 us)
Sparse Core Ops, SparseCore 0:
  90.9 103.8 all-gather.1
  348.6 39.8 reduce-scatter.4
  391.5 65.8 reduce-scatter.6
  459.5 23.0 reduce-scatter.10
  484.7 38.5 reduce-scatter.8
